TPU v7x, 256 devices: a whole 4x4x8 slice. The times are simulated.
256 devices in a mesh: base: 32 (over z_lo, x, core), band: 8 (over z_hi, y).
Axes of the slice: x: 4, y: 4, z: 8 (z_hi: 2, z_lo: 4; z = z_hi * 4 + z_lo), core: 2. Of those that a mesh axis runs over, the one named last changes fastest.
Arguments:
- coherency: float32 [16, 16, 8, 8192], P('band', None, None, 'base'), may hold values from -1.5 to 1.5
- observed: float32 [16, 8, 8192], P('band', None, 'base'), may hold values from -6 to 6
- jones_deviation: float32 [16, 16, 8, 512], P('band', None, None, 'base'), may hold values from -1.8 to 1.8
- antenna_first: int32 [8192], P('base'), may hold values from 0 to 511, as said below
- antenna_second: int32 [8192], P('base'), may hold values from 0 to 511, as said below
Outputs:
- jones: float32 [16, 16, 8, 512], P('band', None, None, 'base')
- residual: float32 [16, 8, 8192], P('band', None, 'base')
Inputs may be any that keep to these rules, and one draw needn't show every extreme that they name: `antenna_first`: every station is the first station of exactly 16 baselines. On every baseline antenna_second differs from antenna_first.
All inputs are finite; a program needn't handle non-finite values.
Results may differ from a plain program's by a relative error of at most 0.0003.
Values sent between devices are 32-bit elements; how exact they have to be, the bound alone decides.
No kernel may reach another device: no remote copies, remote signals or barrier semaphores. Data moves between devices by JAX's collectives and lax.ppermute only.
A program may use at most 64 MiB of HBM per device.

v0:
```python
import jax
import jax.numpy as jnp
from jax import lax
from jax.sharding import PartitionSpec as P

ITERS = 3


step_gain = 1.2
penalty_gain = 0.25


def expand_matrix(packed):
    return [
        [(packed[..., 0, :], packed[..., 1, :]), (packed[..., 2, :], packed[..., 3, :])],
        [(packed[..., 4, :], packed[..., 5, :]), (packed[..., 6, :], packed[..., 7, :])],
    ]


def pack_matrix(matrix):
    return jnp.stack(
        [
            matrix[0][0][0],
            matrix[0][0][1],
            matrix[0][1][0],
            matrix[0][1][1],
            matrix[1][0][0],
            matrix[1][0][1],
            matrix[1][1][0],
            matrix[1][1][1],
        ],
        axis=-2,
    )


def complex_mul(first_term, second_term):
    return (
        first_term[0] * second_term[0] - first_term[1] * second_term[1],
        first_term[0] * second_term[1] + first_term[1] * second_term[0],
    )


def complex_add(first_term, second_term):
    return (first_term[0] + second_term[0], first_term[1] + second_term[1])


def element_of(matrix, i, j, adjoint):
    if adjoint:
        return (matrix[j][i][0], -matrix[j][i][1])
    return matrix[i][j]


def matrix_product(first_factor, second_factor, adjoint_first=False, adjoint_second=False):
    result_rows = []
    for i in range(2):
        row_items = []
        for j in range(2):
            row_items.append(
                complex_add(
                    complex_mul(
                        element_of(first_factor, i, 0, adjoint_first),
                        element_of(second_factor, 0, j, adjoint_second),
                    ),
                    complex_mul(
                        element_of(first_factor, i, 1, adjoint_first),
                        element_of(second_factor, 1, j, adjoint_second),
                    ),
                )
            )
        result_rows.append(row_items)
    return result_rows


def fit_basis(band_count):
    positions = (2.0 * jnp.arange(band_count, dtype=jnp.float32) + 1.0) / band_count - 1.0
    columns = []
    for power in range(4):
        vector = positions**power
        for earlier in columns:
            vector = vector - jnp.sum(earlier * vector) * earlier
        vector = vector / jnp.sqrt(jnp.sum(vector * vector))
        columns.append(vector)
    return jnp.stack(columns, axis=1)


def local_gradients(
    leading_rows, trailing_rows, coherency, observed, antenna_first, antenna_second, station_number
):
    leading_jones = expand_matrix(leading_rows)
    trailing_jones = expand_matrix(trailing_rows)
    sky = expand_matrix(coherency)
    model = pack_matrix(
        matrix_product(leading_jones, matrix_product(sky, trailing_jones, adjoint_second=True))
    )
    residual = observed - jnp.sum(model, axis=1)
    resid_parts = expand_matrix(residual[:, None])
    gradient_leading = pack_matrix(
        matrix_product(resid_parts, matrix_product(trailing_jones, sky, adjoint_second=True))
    )
    gradient_trailing = pack_matrix(
        matrix_product(resid_parts, matrix_product(leading_jones, sky), adjoint_first=True)
    )
    shape_out = (coherency.shape[0], coherency.shape[1], 8, station_number)
    gradient_list = (
        jnp.zeros(shape_out, jnp.float32)
        .at[:, :, :, antenna_first]
        .add(gradient_leading)
        .at[:, :, :, antenna_second]
        .add(gradient_trailing)
    )
    return (gradient_list, residual)


def per_device(coherency, observed, jones_deviation, antenna_first, antenna_second):
    highest = lax.Precision.HIGHEST
    base_count = lax.axis_size("base")
    band_count = lax.axis_size("band")
    sub_dev = coherency.shape[0]
    base_dev = coherency.shape[-1]
    own_stations = jones_deviation.shape[-1]
    station_number = own_stations * base_count
    baseline_count = base_dev * base_count
    step_size = step_gain * station_number / baseline_count
    penalty = penalty_gain * baseline_count / station_number
    poly_basis = fit_basis(sub_dev * band_count)
    local_basis = lax.dynamic_slice_in_dim(poly_basis, lax.axis_index("band") * sub_dev, sub_dev, 0)
    identity = jnp.array([1.0, 0.0, 0.0, 0.0, 0.0, 0.0, 1.0, 0.0], dtype=jnp.float32)[:, None]
    jones_current = identity + jones_deviation
    consensus = jones_current
    dual_var = jnp.zeros_like(jones_current)
    residual = None
    for iteration in range(ITERS):
        every_station = lax.all_gather(jones_current, "base", axis=3, tiled=True)
        leading_rows = jnp.take(every_station, antenna_first, axis=3)
        trailing_rows = jnp.take(every_station, antenna_second, axis=3)
        local_terms, residual = local_gradients(
            leading_rows,
            trailing_rows,
            coherency,
            observed,
            antenna_first,
            antenna_second,
            station_number,
        )
        station_gradients = lax.psum_scatter(local_terms, "base", scatter_dimension=3, tiled=True)
        jones_current = jones_current + step_size * (
            station_gradients - dual_var - penalty * (jones_current - consensus)
        )
        if iteration + 1 < ITERS:
            target = jones_current + dual_var / penalty
            partial_fit = jnp.einsum("fm,fkcs->mkcs", local_basis, target, precision=highest)
            coefficients = lax.psum(partial_fit, "band")
            consensus = jnp.einsum("fm,mkcs->fkcs", local_basis, coefficients, precision=highest)
            dual_var = dual_var + penalty * (jones_current - consensus)
    return (jones_current, residual)


def solution(mesh):
    return jax.shard_map(
        per_device,
        mesh=mesh,
        in_specs=(
            P("band", None, None, "base"),
            P("band", None, "base"),
            P("band", None, None, "base"),
            P("base"),
            P("base"),
        ),
        out_specs=(P("band", None, None, "base"), P("band", None, "base")),
        check_vma=False,
    )
```

profile of v0, /device:TPU:1, one launch (start us, length us, event | category | flops | bytes accessed | tf_op | source)
XLA Modules:
  0.0 905.2 jit_solution(18151119137562045267)
XLA Ops:
  11.1 59.7 %all_gather.9 = f32[2,16,8,512]{1,2,0,3:T(8,128)S(1)} all-gather(f32[2,16,8,16]{1,2,0,3:T(8,128)S(1)} %copy.508), channel_id=1, replica_groups=mesh['base'=32,'band'=8] {'base'}, dimensions={3}, use_global_device_ids=true | all-gather | bytes 540672 | tf_op jit(solution)/shard_map/all_gather | solution.py:133
  73.0 3.0 gather_fusion
  77.3 3.0 gather_fusion.1
  93.1 31.2 %scatter_fusion = f32[2,16,8,512]{1,2,3,0:T(8,128)} fusion(f32[2,16,8,512]{1,2,3,0:T(8,128)} %broadcast.414.clone, s32[256]{0:T(256)S(1)} %compare_select_fusion.1, f32[256,2,16,8]{2,3,1,0:T(8,128)} %copy.539), kind=kCustom, calls=%fused_computation.6 | custom fusion | flops 65536 | bytes 787456 | tf_op jit(solution)/shard_map/scatter-add | solution.py:107
  124.3 27.8 %scatter_fusion.1 = f32[2,16,8,512]{1,2,3,0:T(8,128)} fusion(f32[2,16,8,512]{1,2,3,0:T(8,128)} %scatter_fusion, s32[256]{0:T(256)S(1)} %compare_select_fusion, f32[256,2,16,8]{2,3,1,0:T(8,128)S(1)} %copy.548), kind=kCustom, calls=%fused_computation.7 | custom fusion | flops 65536 | bytes 787456 | tf_op jit(solution)/shard_map/scatter-add | solution.py:109
  152.0 4.5 copy.549
  164.4 134.4 %reduce-scatter.4.cloned.1.call-done = f32[2,16,8,16]{1,2,0,3:T(8,128)} async-done(((f32[2,16,8,512]{1,2,0,3:T(8,128)}), f32[2,16,8,16]{1,2,0,3:T(8,128)}) %reduce-scatter.4.cloned.1.call-update) | async-done | bytes 16400 | tf_op jit(solution)/shard_map/reduce_scatter | solution.py:145
  300.0 60.3 %all_gather.10 = f32[2,16,8,512]{1,2,0,3:T(8,128)S(1)} all-gather(f32[2,16,8,16]{1,2,0,3:T(8,128)S(1)} %copy.551), channel_id=1, replica_groups=mesh['base'=32,'band'=8] {'base'}, dimensions={3}, use_global_device_ids=true | all-gather | bytes 540672 | tf_op jit(solution)/shard_map/all_gather | solution.py:133
  362.5 4.4 gather_fusion.3
  366.9 3.0 gather_fusion.2
  387.7 31.2 %scatter_fusion.2 = f32[2,16,8,512]{1,2,3,0:T(8,128)} fusion(f32[2,16,8,512]{1,2,3,0:T(8,128)} %broadcast.414.clone.1, s32[256]{0:T(256)S(1)} %copy-done.28, f32[256,2,16,8]{2,3,1,0:T(8,128)} %copy.574), kind=kCustom, calls=%fused_computation.8 | custom fusion | flops 65536 | bytes 787456 | tf_op jit(solution)/shard_map/scatter-add | solution.py:107
  418.9 27.8 %scatter_fusion.3 = f32[2,16,8,512]{1,2,3,0:T(8,128)} fusion(f32[2,16,8,512]{1,2,3,0:T(8,128)} %scatter_fusion.2, s32[256]{0:T(256)S(1)} %copy-done.25, f32[256,2,16,8]{2,3,1,0:T(8,128)S(1)} %copy.583), kind=kCustom, calls=%fused_computation.9 | custom fusion | flops 65536 | bytes 787456 | tf_op jit(solution)/shard_map/scatter-add | solution.py:109
  446.7 4.5 copy.584
  458.9 47.8 %psum.14 = f32[4,16,8,16]{3,0,2,1:T(4,128)S(1)} all-reduce(f32[4,16,8,16]{3,0,2,1:T(4,128)S(1)} %fusion.5), channel_id=1, replica_groups=mesh['base'=32,'band'=8] {'band'}, use_global_device_ids=true, to_apply=%region_17.19 | all-reduce | flops 8192 | bytes 65536 | tf_op jit(solution)/shard_map/psum | solution.py:152
  507.5 85.1 %reduce-scatter.6.cloned.1.call-done = f32[2,16,8,16]{1,2,0,3:T(8,128)} async-done(((f32[2,16,8,512]{1,2,0,3:T(8,128)}), f32[2,16,8,16]{1,2,0,3:T(8,128)}) %reduce-scatter.6.cloned.1.call-update) | async-done | bytes 16400 | tf_op jit(solution)/shard_map/reduce_scatter | solution.py:145
  594.4 69.1 %all_gather.11 = f32[2,16,8,512]{1,2,0,3:T(8,128)S(1)} all-gather(f32[2,16,8,16]{1,2,0,3:T(8,128)S(1)} %copy.589), channel_id=1, replica_groups=mesh['base'=32,'band'=8] {'base'}, dimensions={3}, use_global_device_ids=true | all-gather | bytes 540672 | tf_op jit(solution)/shard_map/all_gather | solution.py:133
  665.7 4.5 gather_fusion.5
  670.2 3.1 gather_fusion.4
  686.9 2.5 copy.612
  691.7 31.2 %scatter_fusion.4 = f32[2,16,8,512]{1,2,3,0:T(8,128)} fusion(f32[2,16,8,512]{1,2,3,0:T(8,128)} %broadcast.414, s32[256]{0:T(256)S(1)} %copy-done.29, f32[256,2,16,8]{2,3,1,0:T(8,128)} %copy.612), kind=kCustom, calls=%fused_computation.10 | custom fusion | flops 65536 | bytes 787456 | tf_op jit(solution)/shard_map/scatter-add | solution.py:107
  722.8 27.8 %scatter_fusion.5 = f32[2,16,8,512]{1,2,3,0:T(8,128)} fusion(f32[2,16,8,512]{1,2,3,0:T(8,128)} %scatter_fusion.4, s32[256]{0:T(256)S(1)} %copy-done.26, f32[256,2,16,8]{2,3,1,0:T(8,128)S(1)} %copy.621), kind=kCustom, calls=%fused_computation.11 | custom fusion | flops 65536 | bytes 787456 | tf_op jit(solution)/shard_map/scatter-add | solution.py:109
  750.6 4.5 copy.622
  756.7 47.1 %psum.15 = f32[4,16,8,16]{3,0,2,1:T(4,128)S(1)} all-reduce(f32[4,16,8,16]{3,0,2,1:T(4,128)S(1)} %fusion.3), channel_id=1, replica_groups=mesh['base'=32,'band'=8] {'band'}, use_global_device_ids=true, to_apply=%region_22.24 | all-reduce | flops 8192 | bytes 65536 | tf_op jit(solution)/shard_map/psum | solution.py:152
  804.6 92.2 %reduce-scatter.8.cloned.1.call-done = f32[2,16,8,16]{1,2,0,3:T(8,128)} async-done(((f32[2,16,8,512]{1,2,0,3:T(8,128)}), f32[2,16,8,16]{1,2,0,3:T(8,128)}) %reduce-scatter.8.cloned.1.call-update) | async-done | bytes 16400 | tf_op jit(solution)/shard_map/reduce_scatter | solution.py:145
  (298 shorter events, 76.7 us)
Async XLA Ops:
  7.2 291.6 %reduce-scatter.4.cloned.1.call-start = ((), (), s32[]{:S(2)}) async-start(), calls=%async_computation.3 | async-start | bytes 4325376 | tf_op jit(solution)/shard_map/reduce_scatter | solution.py:145
  7.9 85.2 %copy-start.27 = (s32[256]{0:T(256)}, s32[256]{0:T(256)S(1)}, u32[]{:S(2)}) copy-start(s32[256]{0:T(256)S(1)} %compare_select_fusion.1) | copy-start | bytes 3076
  8.6 364.8 %copy-start.41 = (pred[256]{0:T(512)(128)(4,1)}, pred[256]{0:T(512)(128)(4,1)S(1)}, u32[]{:S(2)}) copy-start(pred[256]{0:T(512)(128)(4,1)S(1)} %compare_and_fusion.1) | copy-start | bytes 772
  9.3 115.0 %copy-start.24 = (s32[256]{0:T(256)}, s32[256]{0:T(256)S(1)}, u32[]{:S(2)}) copy-start(s32[256]{0:T(256)S(1)} %compare_select_fusion) | copy-start | bytes 3076
  10.0 362.4 %copy-start.43 = (pred[256]{0:T(512)(128)(4,1)}, pred[256]{0:T(512)(128)(4,1)S(1)}, u32[]{:S(2)}) copy-start(pred[256]{0:T(512)(128)(4,1)S(1)} %compare_and_fusion) | copy-start | bytes 772
  70.8 6.3 copy-start.6
  73.0 289.5 %copy-start.38 = (s32[1024]{0:T(1024)}, s32[1024]{0:T(1024)S(1)}, u32[]{:S(2)}) copy-start(s32[1024]{0:T(1024)S(1)} %get-tuple-element.202) | copy-start | bytes 12292
  73.0 293.9 %copy-start.37 = (s32[1024]{0:T(1024)}, s32[1024]{0:T(1024)S(1)}, u32[]{:S(2)}) copy-start(s32[1024]{0:T(1024)S(1)} %get-tuple-element.203) | copy-start | bytes 12292
  77.0 4.8 copy-start.36
  156.5 143.3 %copy-start.5 = (f32[2,16,8,16]{3,2,1,0:T(8,128)S(1)}, f32[2,16,8,16]{3,2,1,0:T(8,128)}, u32[]{:S(2)}) copy-start(f32[2,16,8,16]{3,2,1,0:T(8,128)} %param.10) | copy-start | bytes 49156
  156.5 143.3 %copy-start.45 = (f32[8]{0:T(128)S(1)}, f32[8]{0:T(128)}, u32[]{:S(2)}) copy-start(f32[8]{0:T(128)} %constant.46.clone) | copy-start | bytes 100
  156.5 436.0 %reduce-scatter.6.cloned.1.call-start = ((), (), s32[]{:S(2)}) async-start(), calls=%async_computation.4 | async-start | bytes 4325376 | tf_op jit(solution)/shard_map/reduce_scatter | solution.py:145
  162.4 200.1 %copy-start.39 = (f32[16]{0:T(128)}, f32[16]{0:T(128)S(1)}, u32[]{:S(2)}) copy-start(f32[16]{0:T(128)S(1)} %get-tuple-element.53) | copy-start | bytes 196
  381.3 6.4 copy-start.28
  382.2 36.7 %copy-start.25 = (s32[256]{0:T(256)S(1)}, s32[256]{0:T(256)}, u32[]{:S(2)}) copy-start(s32[256]{0:T(256)} %copy-done.24) | copy-start | bytes 3076
  451.2 445.6 %reduce-scatter.8.cloned.1.call-start = ((), (), s32[]{:S(2)}) async-start(), calls=%async_computation.5 | async-start | bytes 4325376 | tf_op jit(solution)/shard_map/reduce_scatter | solution.py:145
  507.5 158.2 %copy-start = (f32[2,16,8,16]{3,0,2,1:T(2,128)}, f32[2,16,8,16]{3,0,2,1:T(2,128)S(1)}, u32[]{:S(2)}) copy-start(f32[2,16,8,16]{3,0,2,1:T(2,128)S(1)} %fusion.12) | copy-start | bytes 49156
  593.6 72.1 %copy-start.2 = (f32[2,16,8,16]{3,2,1,0:T(8,128)}, f32[2,16,8,16]{3,2,1,0:T(8,128)S(1)}, u32[]{:S(2)}) copy-start(f32[2,16,8,16]{3,2,1,0:T(8,128)S(1)} %copy.588) | copy-start | bytes 49156
  663.5 12.4 %copy-start.44 = (pred[256]{0:T(512)(128)(4,1)S(1)}, pred[256]{0:T(512)(128)(4,1)}, u32[]{:S(2)}) copy-start(pred[256]{0:T(512)(128)(4,1)} %copy-done.43) | copy-start | bytes 772
  665.7 11.2 %copy-start.42 = (pred[256]{0:T(512)(128)(4,1)S(1)}, pred[256]{0:T(512)(128)(4,1)}, u32[]{:S(2)}) copy-start(pred[256]{0:T(512)(128)(4,1)} %copy-done.41) | copy-start | bytes 772
  685.3 6.3 copy-start.29
  686.2 36.7 %copy-start.26 = (s32[256]{0:T(256)S(1)}, s32[256]{0:T(256)}, u32[]{:S(2)}) copy-start(s32[256]{0:T(256)} %copy-done.24) | copy-start | bytes 3076
  755.1 142.6 %copy-start.1 = (f32[2,16,8,16]{3,0,2,1:T(2,128)S(1)}, f32[2,16,8,16]{3,0,2,1:T(2,128)}, u32[]{:S(2)}) copy-start(f32[2,16,8,16]{3,0,2,1:T(2,128)} %copy-done) | copy-start | bytes 49156
  755.1 142.6 %copy-start.3 = (f32[2,16,8,16]{3,2,1,0:T(8,128)S(1)}, f32[2,16,8,16]{3,2,1,0:T(8,128)}, u32[]{:S(2)}) copy-start(f32[2,16,8,16]{3,2,1,0:T(8,128)} %copy-done.2) | copy-start | bytes 49156
  (25 other events, 67.7 us)
Sparse Core Ops, SparseCore 0:
  156.7 142.0 reduce-scatter.3
  451.3 141.2 reduce-scatter.5
  755.3 141.4 reduce-scatter.7
where the time goes:
time: 918 us; the launch traced here: 905 us
  waiting for transfers between devices  312 us (34%)
  blocking collectives  284 us (31%)
  other arithmetic  199 us (22%)
  local copies, waits for them, and re-layouts  88.6 us (10%)
  between operations  19.2 us (2%)
    reduce_scatter x3, waiting for transfers between devices, per_device(): lax.psum_scatter(local_terms, 'base', scatter_dimension=3, tiled=True)  312 us
    all_gather x3, blocking collectives, per_device(): every_station = lax.all_gather(jones_current, 'base', axis=3, tiled=True)  189 us
    scatter-add x6, other arithmetic, local_gradients(): gradient_list = jnp.zeros(shape_out, jnp.float32).at[:, :, :, antenna_fir...  177 us
    psum x2, blocking collectives, per_device(): coefficients = lax.psum(partial_fit, 'band')  94.9 us
  transfers between devices with their start and end apart: 3, of which 3 were waited for; matrix products, arithmetic and copies ran while one was open for 2% of the time, Pallas kernels for 0%

commit v1 on v0

v1 whole, which is shorter than its diff:
```python
import functools

import jax
import jax.numpy as jnp
import numpy as np
from jax import lax
from jax.experimental import pallas as pl
from jax.experimental.pallas import tpu as pltpu
from jax.sharding import PartitionSpec as P

ITERS = 3
step_gain = 1.2
penalty_gain = 0.25
LANES = 128


def fit_basis(band_count):
    positions = ((2.0 * np.arange(band_count) + 1.0) / band_count - 1.0).astype(np.float32)
    columns = []
    for power in range(4):
        vector = positions**power
        for earlier in columns:
            vector = vector - np.sum(earlier * vector) * earlier
        vector = vector / np.sqrt(np.sum(vector * vector))
        columns.append(vector.astype(np.float32))
    return np.stack(columns, axis=1)


def split(parts):
    return [[(parts[0], parts[1]), (parts[2], parts[3])], [(parts[4], parts[5]), (parts[6], parts[7])]]


def join(matrix):
    return [matrix[i][j][part] for i in range(2) for j in range(2) for part in range(2)]


def element_of(matrix, i, j, adjoint):
    if adjoint:
        return (matrix[j][i][0], -matrix[j][i][1])
    return matrix[i][j]


def product(first, second, adjoint_first=False, adjoint_second=False):
    first, second = split(first), split(second)
    rows = []
    for i in range(2):
        row = []
        for j in range(2):
            a = element_of(first, i, 0, adjoint_first)
            b = element_of(second, 0, j, adjoint_second)
            c = element_of(first, i, 1, adjoint_first)
            d = element_of(second, 1, j, adjoint_second)
            row.append(
                (
                    a[0] * b[0] - a[1] * b[1] + (c[0] * d[0] - c[1] * d[1]),
                    a[0] * b[1] + a[1] * b[0] + (c[0] * d[1] + c[1] * d[0]),
                )
            )
        rows.append(row)
    return join(rows)


def pick(pieces, rows, low, group):
    value = jnp.take_along_axis(pieces[0][rows, :], low, axis=1)
    for j in range(1, 4):
        value = jnp.where(group == j, jnp.take_along_axis(pieces[j][rows, :], low, axis=1), value)
    return value


def iteration_kernel(dirs, core_ref, j0, j1, j2, j3, own_sky, other_sky, seen, place, column, g0, g1, g2, g3, resid, grads, trail, lead):
    core = core_ref[0]
    pieces = (j0, j1, j2, j3)
    half = own_sky.shape[2]
    count = 2 * half
    dir_groups = dirs // 8
    for h in range(count // LANES):
        lanes = slice(h * LANES, (h + 1) * LANES)
        inside = (h * LANES) % half
        first = jnp.broadcast_to(place[0:1, lanes], (8, LANES))
        second = jnp.broadcast_to(place[1:2, lanes], (8, LANES))
        first_low, first_group = first & (LANES - 1), first >> 7
        second_low, second_group = second & (LANES - 1), second >> 7
        total = None
        for g in range(dir_groups):
            rows = [slice(c * dirs + 8 * g, c * dirs + 8 * g + 8) for c in range(8)]
            leading = [pick(pieces, r, first_low, first_group) for r in rows]
            trailing = [pick(pieces, r, second_low, second_group) for r in rows]
            source = own_sky.at[core] if h * LANES < half else other_sky
            sky = [source[r, inside : inside + LANES] for r in rows]
            forward = product(leading, sky)
            model = product(forward, trailing, adjoint_second=True)
            backward = product(trailing, sky, adjoint_second=True)
            for c in range(8):
                lead[rows[c], lanes] = forward[c]
                trail[rows[c], lanes] = backward[c]
            total = model if total is None else [a + b for a, b in zip(total, model)]
        for c in range(8):
            resid[c : c + 1, lanes] = seen[c : c + 1, lanes] - jnp.sum(total[c], axis=0, keepdims=True)
    for h in range(count // LANES):
        lanes = slice(h * LANES, (h + 1) * LANES)
        left = [jnp.broadcast_to(resid[c : c + 1, lanes], (8, LANES)) for c in range(8)]
        for g in range(dir_groups):
            rows = [slice(c * dirs + 8 * g, c * dirs + 8 * g + 8) for c in range(8)]
            up = product(left, [trail[r, lanes] for r in rows])
            down = product(left, [lead[r, lanes] for r in rows], adjoint_first=True)
            for c in range(8):
                grads[rows[c], lanes] = up[c]
                grads[rows[c], count + h * LANES : count + (h + 1) * LANES] = down[c]
    value = grads[...]
    high = value.astype(jnp.bfloat16)
    low = (value - high.astype(jnp.float32)).astype(jnp.bfloat16)
    both = jnp.concatenate([high, low], axis=0)
    where = column[...]
    outs = (g0, g1, g2, g3)
    stations = lax.broadcasted_iota(jnp.int32, (2 * count, 4 * LANES), 1)
    chosen = jnp.where(where == stations, 1.0, 0.0).astype(jnp.bfloat16)
    result = jnp.dot(both, chosen, preferred_element_type=jnp.float32)
    half_rows = value.shape[0]
    result = result[:half_rows] + result[half_rows:]
    for j in range(4):
        outs[j][...] = result[:, j * LANES : (j + 1) * LANES]


def iterate(core, pieces, own_sky, other_sky, seen, place, column):
    rows = pieces[0].shape[0]
    count = place.shape[1]
    dirs = rows // 8
    smem = pl.BlockSpec(memory_space=pltpu.SMEM)
    vmem = pl.BlockSpec(memory_space=pltpu.VMEM)
    piece = jax.ShapeDtypeStruct((rows, LANES), jnp.float32)
    return pl.pallas_call(
        functools.partial(iteration_kernel, dirs),
        out_shape=[piece] * 4 + [jax.ShapeDtypeStruct((8, count), jnp.float32)],
        in_specs=[smem] + [vmem] * 9,
        out_specs=[vmem] * 5,
        scratch_shapes=[
            pltpu.VMEM((rows, 2 * count), jnp.float32),
            pltpu.VMEM((rows, count), jnp.float32),
            pltpu.VMEM((rows, count), jnp.float32),
        ],
        compiler_params=pltpu.CompilerParams(vmem_limit_bytes=32 * 2**20),
        cost_estimate=pl.CostEstimate(flops=4 * 2**27, bytes_accessed=2**21, transcendentals=0),
    )(core, *pieces, own_sky, other_sky, seen, place, column)


def per_device(coherency, observed, jones_deviation, antenna_first, antenna_second):
    base_count = lax.axis_size("base")
    band_count = lax.axis_size("band")
    sub_dev, dirs = coherency.shape[:2]
    base_dev = coherency.shape[-1]
    own_stations = jones_deviation.shape[-1]
    station_number = own_stations * base_count
    baseline_count = base_dev * base_count
    step_size = step_gain * station_number / baseline_count
    penalty = penalty_gain * baseline_count / station_number
    basis = fit_basis(sub_dev * band_count)
    rows = 8 * dirs
    share = rows // 4

    me = lax.axis_index("base")
    core, x, z = me & 1, (me >> 1) & 3, me >> 3
    band = lax.axis_index("band")

    def base_swap(value, mask):
        return lax.ppermute(value, "base", [(i, i ^ mask) for i in range(base_count)])

    def band_swap(value, mask):
        return lax.ppermute(value, "band", [(i, i ^ mask) for i in range(band_count)])

    def along_x(values):
        return [base_swap(values[k - 1], 2 * k) for k in (1, 2, 3)]

    def along_z(values):
        return [base_swap(values[k - 1], 8 * k) for k in (1, 2, 3)]

    def mine_of(value):
        return jnp.where(core == 0, value[0], value[1])

    def theirs_of(value):
        return jnp.where(core == 0, value[1], value[0])

    turned = jones_deviation.transpose(0, 3, 2, 1).reshape(sub_dev, own_stations, rows)
    identity = jnp.repeat(jnp.array([1.0, 0, 0, 0, 0, 0, 1.0, 0], jnp.float32), dirs)
    turned = turned + identity
    mine, theirs = mine_of(turned), base_swap(theirs_of(turned), 1)
    chip = jnp.where(core == 0, jnp.concatenate([mine, theirs]), jnp.concatenate([theirs, mine]))
    planes = [chip] + along_z([chip] * 3)
    ordered = [jnp.where(z & 1 == 0, planes[a], planes[a ^ 1]) for a in range(4)]
    ordered = [jnp.where(z & 2 == 0, ordered[a], ordered[a ^ 2]) for a in range(4)]
    jones = jnp.concatenate(ordered).T

    pairs = jnp.stack([antenna_first, antenna_second])
    pairs = jnp.concatenate([pairs, base_swap(pairs, 1)], axis=1)
    place = ((((pairs >> 5) & 3) ^ x) << 7) | ((pairs >> 7) << 5) | (pairs & 31)
    column = place.reshape(-1, 1)

    sky = coherency.transpose(0, 2, 1, 3).reshape(sub_dev, rows, base_dev)
    other_sky = base_swap(theirs_of(sky), 1)
    seen = jnp.concatenate([mine_of(observed), base_swap(theirs_of(observed), 1)], axis=1)

    share_rows = jnp.arange(rows)[:, None] // share == z
    core_scalar = core.astype(jnp.int32).reshape(1)
    own_basis = lax.dynamic_slice_in_dim(jnp.asarray(basis), 2 * band + core, 1, 0)[0]
    next_basis = lax.dynamic_slice_in_dim(jnp.asarray(basis), 2 * band + 1 - core, 1, 0)[0]
    far_basis = lax.dynamic_slice_in_dim(jnp.asarray(basis), 2 * (band ^ 4) + core, 1, 0)[0]

    def fit(target):
        beside = base_swap(target, 1)
        partial = own_basis[:, None, None] * target + next_basis[:, None, None] * beside
        for mask in (1, 3):
            partial = partial + band_swap(partial, mask)
        sent = band_swap(jnp.sum(far_basis[:, None, None] * partial, axis=0), 4)
        return jnp.sum(own_basis[:, None, None] * partial, axis=0) + sent

    dual = jnp.zeros((share, LANES), jnp.float32)
    correction = None
    residual = None
    for iteration in range(ITERS):
        pieces = [jones] + along_x([jones] * 3)
        *terms, residual = iterate(core_scalar, pieces, sky, other_sky, seen, place, column)
        received = along_x(terms[1:])
        if iteration:
            held = lax.dynamic_slice_in_dim(jones, z * share, share, 0)
            consensus = fit(held + dual / penalty)
            dual = dual + penalty * (held - consensus)
            correction = dual + penalty * (held - consensus)
            spread = jnp.where(share_rows, jnp.concatenate([correction] * 4), 0.0)
            summed = terms[0] - spread + received[0] + received[1] + received[2]
        else:
            summed = terms[0] + received[0] + received[1] + received[2]
        if iteration + 1 < ITERS:
            others = along_z([summed] * 3)
            jones = jones + step_size * (summed + others[0] + others[1] + others[2])
    per_station = 2 * own_stations
    turned_sum = summed.T
    parts = [lax.dynamic_slice_in_dim(turned_sum, (z ^ k) * per_station, per_station, 0) for k in range(4)]
    others = along_z(parts[1:])
    last = lax.dynamic_slice_in_dim(jones.T, z * per_station, per_station, 0)
    last = last + step_size * (parts[0] + others[0] + others[1] + others[2])
    last = last.reshape(2, own_stations, rows)
    kept, given = mine_of(last), base_swap(theirs_of(last), 1)
    both = jnp.where(core == 0, jnp.stack([kept, given]), jnp.stack([given, kept]))
    jones_out = both.reshape(sub_dev, own_stations, 8, dirs).transpose(0, 3, 2, 1)
    here, there = residual[:, :base_dev], base_swap(residual[:, base_dev:], 1)
    residual_out = jnp.where(core == 0, jnp.stack([here, there]), jnp.stack([there, here]))
    return (jones_out, residual_out)


def solution(mesh):
    return jax.shard_map(
        per_device,
        mesh=mesh,
        in_specs=(
            P("band", None, None, "base"),
            P("band", None, "base"),
            P("band", None, None, "base"),
            P("base"),
            P("base"),
        ),
        out_specs=(P("band", None, None, "base"), P("band", None, "base")),
        check_vma=False,
    )
```

time: 918 us -> 115 us (0.13); the launches traced: 905 us -> 114 us
  blocking collectives: 284 us -> 0 us
  waiting for transfers between devices: 312 us -> 29.2 us
  other arithmetic: 199 us -> 2.46 us
  local copies, waits for them, and re-layouts: 88.6 us -> 4.03 us
  starting transfers between devices: 0.12 us -> 73.6 us
  between operations: 19.2 us -> 0.97 us
    reduce_scatter x3 -> x0, waiting for transfers between devices: 312 us -> none  [per_device(): lax.psum_scatter(local_terms, 'base', scatter_dimension=3, tiled=True)]
    all_gather x3 -> x0, blocking collectives: 189 us -> none  [per_device(): every_station = lax.all_gather(jones_current, 'base', axis=3, tiled=True)]
    scatter-add x6 -> x0, other arithmetic: 177 us -> none  [local_gradients(): gradient_list = jnp.zeros(shape_out, jnp.float32).at[:, :, :, antenna_fir...]
    psum x2 -> x0, blocking collectives: 94.9 us -> none  [per_device(): coefficients = lax.psum(partial_fit, 'band')]
    ppermute x0 -> x44, starting transfers between devices: none -> 73.6 us  [the longest x38 60.4 us: base_swap(): lax.ppermute(value, 'base', [(i, i ^ mask) for i in range(base_count)])]
    gather x12 -> x0, local copies, waits for them, and re-layouts: 30 us -> none  [the longest x6 17.9 us: per_device(): trailing_rows = jnp.take(every_station, antenna_second, axis=3)]
    ppermute x0 -> x44, waiting for transfers between devices: none -> 29.2 us  [the longest x38 24.3 us: base_swap(): lax.ppermute(value, 'base', [(i, i ^ mask) for i in range(base_count)])]
    another operation x16 -> x3, local copies, waits for them, and re-layouts: 20.5 us -> 0.05 us  [the longest x2 0.05 us: per_device(): jnp.stack([kept, given])]
  transfers between devices with their start and end apart: 3 -> 44, of which waited for: 3 -> 21; matrix products, arithmetic and copies ran while one was open for 2% -> 2% of each run, Pallas kernels for 0% -> 2%
where the time goes in v1:
time: 115 us; the launch traced here: 114 us
  starting transfers between devices  73.6 us (64%)
  waiting for transfers between devices  29.2 us (25%)
  local copies, waits for them, and re-layouts  4.03 us (4%)
  Pallas kernels  4.03 us (4%)
  other arithmetic  2.46 us (2%)
    ppermute x38, starting transfers between devices, base_swap(): lax.ppermute(value, 'base', [(i, i ^ mask) for i in range(base_count)])  60.4 us
    ppermute x38, waiting for transfers between devices, base_swap(): lax.ppermute(value, 'base', [(i, i ^ mask) for i in range(base_count)])  24.3 us
    ppermute x6, starting transfers between devices, band_swap(): lax.ppermute(value, 'band', [(i, i ^ mask) for i in range(band_count)])  13.2 us
    ppermute x6, waiting for transfers between devices, band_swap(): lax.ppermute(value, 'band', [(i, i ^ mask) for i in range(band_count)])  4.93 us
    pallas_call x3, Pallas kernels, iterate(): pl.pallas_call(functools.partial(iteration_kernel, dirs), out_shape=[piec...  4.03 us
  transfers between devices with their start and end apart: 44, of which 21 were waited for; matrix products, arithmetic and copies ran while one was open for 2% of the time, Pallas kernels for 2%

profile of v1, /device:TPU:1, one launch (start us, length us, event | category | flops | bytes accessed | tf_op | source)
XLA Modules:
  0.0 114.3 jit_solution(16051034867661379386)
XLA Ops:
  2.5 3.3 %collective-permute-start = (f32[16,128]{1,0:T(8,128)S(1)}, f32[16,128]{1,0:T(8,128)S(1)}, u32[]{:S(2)}, u32[]{:S(2)}) collective-permute-start(f32[16,128]{1,0:T(8,128)S(1)} %get-tuple-element.50), channel_id=1, source_target_pairs={{0,8},{8,0},{16,24},{24,16},{32,40},{40,32},{48,56},{56,48},{64,72... | collective-permute-start | bytes 24584 | tf_op jit(solution)/shard_map/ppermute | solution.py:165
  8.4 2.9 %collective-permute-start.2 = (f32[32,128]{0,1:T(8,128)S(1)}, f32[32,128]{0,1:T(8,128)S(1)}, u32[]{:S(2)}, u32[]{:S(2)}) collective-permute-start(f32[32,128]{0,1:T(8,128)S(1)} %broadcast_select_fusion), channel_id=1, source_target_pairs={{0,128},{8,136},{16,144},{24,152},{32,160},{40,168},{48,176},{56,1... | collective-permute-start | bytes 49160 | tf_op jit(solution)/shard_map/ppermute | solution.py:165
  13.0 3.3 %collective-permute-done.3 = f32[32,128]{0,1:T(8,128)S(1)} collective-permute-done((f32[32,128]{0,1:T(8,128)S(1)}, f32[32,128]{0,1:T(8,128)S(1)}, u32[]{:S(2)}, u32[]{:S(2)}) %collective-permute-start.3) | collective-permute-done | bytes 16416 | tf_op jit(solution)/shard_map/ppermute | solution.py:165
  17.8 2.5 %collective-permute-start.5 = (f32[128,128]{1,0:T(8,128)S(1)}, f32[128,128]{1,0:T(8,128)S(1)}, u32[]{:S(2)}, u32[]{:S(2)}) collective-permute-start(f32[128,128]{1,0:T(8,128)S(1)} %maximum_bitcast_fusion.j0), channel_id=1, source_target_pairs={{0,32},{8,40},{16,48},{24,56},{32,0},{40,8},{48,16},{56,24},{64,96... | collective-permute-start | bytes 196616 | tf_op jit(solution)/shard_map/ppermute | solution.py:165
  20.4 2.1 %collective-permute-done.5.j2 = f32[128,128]{1,0:T(8,128)S(1)} collective-permute-done((f32[128,128]{1,0:T(8,128)S(1)}, f32[128,128]{1,0:T(8,128)S(1)}, u32[]{:S(2)}, u32[]{:S(2)}) %collective-permute-start.5) | collective-permute-done | bytes 65568 | tf_op jit(solution)/shard_map/ppermute | solution.py:165
  22.6 2.3 %collective-permute-done.6.j3 = f32[128,128]{1,0:T(8,128)S(1)} collective-permute-done((f32[128,128]{1,0:T(8,128)S(1)}, f32[128,128]{1,0:T(8,128)S(1)}, u32[]{:S(2)}, u32[]{:S(2)}) %collective-permute-start.6) | collective-permute-done | bytes 65568 | tf_op jit(solution)/shard_map/ppermute | solution.py:165
  26.9 2.6 %collective-permute-start.10 = (f32[128,128]{1,0:T(8,128)S(1)}, f32[128,128]{1,0:T(8,128)S(1)}, u32[]{:S(2)}, u32[]{:S(2)}) collective-permute-start(f32[128,128]{1,0:T(8,128)S(1)} %get-tuple-element.16), channel_id=1, source_target_pairs={{0,16},{8,24},{16,0},{24,8},{32,48},{40,56},{48,32},{56,40},{64,80... | collective-permute-start | bytes 196616 | tf_op jit(solution)/shard_map/ppermute | solution.py:165
  29.5 1.8 %collective-permute-done.12 = f32[128,128]{1,0:T(8,128)S(1)} collective-permute-done((f32[128,128]{1,0:T(8,128)S(1)}, f32[128,128]{1,0:T(8,128)S(1)}, u32[]{:S(2)}, u32[]{:S(2)}) %collective-permute-start.12) | collective-permute-done | bytes 65568 | tf_op jit(solution)/shard_map/ppermute | solution.py:165
  32.8 1.8 %collective-permute-start.14 = (f32[128,128]{1,0:T(8,128)S(1)}, f32[128,128]{1,0:T(8,128)S(1)}, u32[]{:S(2)}, u32[]{:S(2)}) collective-permute-start(f32[128,128]{1,0:T(8,128)S(1)} %add_add_fusion), channel_id=1, source_target_pairs={{0,128},{8,136},{16,144},{24,152},{32,160},{40,168},{48,176},{56,1... | collective-permute-start | bytes 196616 | tf_op jit(solution)/shard_map/ppermute | solution.py:165
  38.3 6.3 %collective-permute-start.19 = (f32[32,128]{1,0:T(8,128)S(1)}, f32[32,128]{1,0:T(8,128)S(1)}, u32[]{:S(2)}, u32[]{:S(2)}) collective-permute-start(f32[32,128]{1,0:T(8,128)S(1)} %constant_dynamic-slice_fusion.3), channel_id=1, source_target_pairs={{0,8},{8,0},{16,24},{24,16},{32,40},{40,32},{48,56},{56,48},{64,72... | collective-permute-start | bytes 49160 | tf_op jit(solution)/shard_map/ppermute | solution.py:165
  46.9 1.8 %collective-permute-done.20 = f32[4,32,128]{2,1,0:T(8,128)S(1)} collective-permute-done((f32[4,32,128]{2,1,0:T(8,128)S(1)}, f32[4,32,128]{2,1,0:T(8,128)S(1)}, u32[]{:S(2)}, u32[]{:S(2)}) %collective-permute-start.20) | collective-permute-done | bytes 65568 | tf_op jit(solution)/shard_map/ppermute | solution.py:168
  48.8 3.0 %collective-permute-start.21 = (f32[4,32,128]{2,1,0:T(8,128)S(1)}, f32[4,32,128]{2,1,0:T(8,128)S(1)}, u32[]{:S(2)}, u32[]{:S(2)}) collective-permute-start(f32[4,32,128]{2,1,0:T(8,128)S(1)} %fusion.17), channel_id=1, source_target_pairs={{0,3},{1,2},{2,1},{3,0},{4,7},{5,6},{6,5},{7,4},{8,11},{9,10},{10,... | collective-permute-start | bytes 196616 | tf_op jit(solution)/shard_map/ppermute | solution.py:168
  52.9 1.8 %collective-permute-start.17 = (f32[128,128]{1,0:T(8,128)S(1)}, f32[128,128]{1,0:T(8,128)S(1)}, u32[]{:S(2)}, u32[]{:S(2)}) collective-permute-start(f32[128,128]{1,0:T(8,128)S(1)} %multiply_add_fusion.3.j0), channel_id=1, source_target_pairs={{0,32},{8,40},{16,48},{24,56},{32,0},{40,8},{48,16},{56,24},{64,96... | collective-permute-start | bytes 196616 | tf_op jit(solution)/shard_map/ppermute | solution.py:165
  55.8 5.0 %collective-permute-start.22 = (f32[32,128]{1,0:T(8,128)S(1)}, f32[32,128]{1,0:T(8,128)S(1)}, u32[]{:S(2)}, u32[]{:S(2)}) collective-permute-start(f32[32,128]{1,0:T(8,128)S(1)} %get-tuple-element.30), channel_id=1, source_target_pairs={{0,4},{1,5},{2,6},{3,7},{4,0},{5,1},{6,2},{7,3},{8,12},{9,13},{10,... | collective-permute-start | bytes 49160 | tf_op jit(solution)/shard_map/ppermute | solution.py:168
  66.6 2.0 %collective-permute-done.24 = f32[128,128]{1,0:T(8,128)S(1)} collective-permute-done((f32[128,128]{1,0:T(8,128)S(1)}, f32[128,128]{1,0:T(8,128)S(1)}, u32[]{:S(2)}, u32[]{:S(2)}) %collective-permute-start.24) | collective-permute-done | bytes 65568 | tf_op jit(solution)/shard_map/ppermute | solution.py:165
  68.7 1.7 %collective-permute-start.28 = (f32[128,128]{1,0:T(8,128)S(1)}, f32[128,128]{1,0:T(8,128)S(1)}, u32[]{:S(2)}, u32[]{:S(2)}) collective-permute-start(f32[128,128]{1,0:T(8,128)S(1)} %fusion.4), channel_id=1, source_target_pairs={{0,192},{8,200},{16,208},{24,216},{32,224},{40,232},{48,240},{56,2... | collective-permute-start | bytes 196616 | tf_op jit(solution)/shard_map/ppermute | solution.py:165
  75.2 5.6 %collective-permute-start.32 = (f32[32,128]{1,0:T(8,128)S(1)}, f32[32,128]{1,0:T(8,128)S(1)}, u32[]{:S(2)}, u32[]{:S(2)}) collective-permute-start(f32[32,128]{1,0:T(8,128)S(1)} %dynamic-slice_add_fusion), channel_id=1, source_target_pairs={{0,8},{8,0},{16,24},{24,16},{32,40},{40,32},{48,56},{56,48},{64,72... | collective-permute-start | bytes 49160 | tf_op jit(solution)/shard_map/ppermute | solution.py:165
  81.8 3.1 %collective-permute-done.33 = f32[4,32,128]{2,1,0:T(8,128)S(1)} collective-permute-done((f32[4,32,128]{2,1,0:T(8,128)S(1)}, f32[4,32,128]{2,1,0:T(8,128)S(1)}, u32[]{:S(2)}, u32[]{:S(2)}) %collective-permute-start.33) | collective-permute-done | bytes 65568 | tf_op jit(solution)/shard_map/ppermute | solution.py:168
  85.8 1.8 %collective-permute-start.30 = (f32[128,128]{1,0:T(8,128)S(1)}, f32[128,128]{1,0:T(8,128)S(1)}, u32[]{:S(2)}, u32[]{:S(2)}) collective-permute-start(f32[128,128]{1,0:T(8,128)S(1)} %multiply_add_fusion.1.j0), channel_id=1, source_target_pairs={{0,32},{8,40},{16,48},{24,56},{32,0},{40,8},{48,16},{56,24},{64,96... | collective-permute-start | bytes 196616 | tf_op jit(solution)/shard_map/ppermute | solution.py:165
  89.5 3.1 %collective-permute-start.35 = (f32[32,128]{1,0:T(8,128)S(1)}, f32[32,128]{1,0:T(8,128)S(1)}, u32[]{:S(2)}, u32[]{:S(2)}) collective-permute-start(f32[32,128]{1,0:T(8,128)S(1)} %get-tuple-element.28), channel_id=1, source_target_pairs={{0,4},{1,5},{2,6},{3,7},{4,0},{5,1},{6,2},{7,3},{8,12},{9,13},{10,... | collective-permute-start | bytes 49160 | tf_op jit(solution)/shard_map/ppermute | solution.py:168
  93.7 1.8 %collective-permute-start.38 = (f32[128,128]{1,0:T(8,128)S(1)}, f32[128,128]{1,0:T(8,128)S(1)}, u32[]{:S(2)}, u32[]{:S(2)}) collective-permute-start(f32[128,128]{1,0:T(8,128)S(1)} %get-tuple-element.26), channel_id=1, source_target_pairs={{0,48},{8,56},{16,32},{24,40},{32,16},{40,24},{48,0},{56,8},{64,11... | collective-permute-start | bytes 196616 | tf_op jit(solution)/shard_map/ppermute | solution.py:165
  100.4 1.7 %collective-permute-start.41 = (f32[32,128]{0,1:T(8,128)S(1)}, f32[32,128]{0,1:T(8,128)S(1)}, u32[]{:S(2)}, u32[]{:S(2)}) collective-permute-start(f32[32,128]{0,1:T(8,128)S(1)} %get-tuple-element.41), channel_id=1, source_target_pairs={{0,192},{8,200},{16,208},{24,216},{32,224},{40,232},{48,240},{56,2... | collective-permute-start | bytes 49160 | tf_op jit(solution)/shard_map/ppermute | solution.py:165
  104.0 5.2 %collective-permute-start.43 = (f32[8,256]{1,0:T(8,128)S(1)}, f32[8,256]{1,0:T(8,128)S(1)}, u32[]{:S(2)}, u32[]{:S(2)}) collective-permute-start(f32[8,256]{1,0:T(8,128)S(1)} %get-tuple-element.44), channel_id=1, source_target_pairs={{0,8},{8,0},{16,24},{24,16},{32,40},{40,32},{48,56},{56,48},{64,72... | collective-permute-start | bytes 24584 | tf_op jit(solution)/shard_map/ppermute | solution.py:165
  109.4 3.3 %collective-permute-start.42 = (f32[16,128]{0,1:T(8,128)S(1)}, f32[16,128]{0,1:T(8,128)S(1)}, u32[]{:S(2)}, u32[]{:S(2)}) collective-permute-start(f32[16,128]{0,1:T(8,128)S(1)} %get-tuple-element.39), channel_id=1, source_target_pairs={{0,8},{8,0},{16,24},{24,16},{32,40},{40,32},{48,56},{56,48},{64,72... | collective-permute-start | bytes 24584 | tf_op jit(solution)/shard_map/ppermute | solution.py:165
  (124 shorter events, 43.5 us)
Async XLA Ops:
  2.5 5.6 %collective-permute-start = (f32[16,128]{1,0:T(8,128)S(1)}, f32[16,128]{1,0:T(8,128)S(1)}, u32[]{:S(2)}, u32[]{:S(2)}) collective-permute-start(f32[16,128]{1,0:T(8,128)S(1)} %get-tuple-element.50), channel_id=1, source_target_pairs={{0,8},{8,0},{16,24},{24,16},{32,40},{40,32},{48,56},{56,48},{64,72... | collective-permute-start | bytes 24584 | tf_op jit(solution)/shard_map/ppermute | solution.py:165
  6.0 18.9 %collective-permute-start.7 = (f32[128,256]{1,0:T(8,128)S(1)}, f32[128,256]{1,0:T(8,128)S(1)}, u32[]{:S(2)}, u32[]{:S(2)}) collective-permute-start(f32[128,256]{1,0:T(8,128)S(1)} %bitcast.65), channel_id=1, source_target_pairs={{0,8},{8,0},{16,24},{24,16},{32,40},{40,32},{48,56},{56,48},{64,72... | collective-permute-start | bytes 393224 | tf_op jit(solution)/shard_map/ppermute | solution.py:165
  7.3 13.2 %collective-permute-start.8 = (f32[8,256]{1,0:T(8,128)S(1)}, f32[8,256]{1,0:T(8,128)S(1)}, u32[]{:S(2)}, u32[]{:S(2)}) collective-permute-start(f32[8,256]{1,0:T(8,128)S(1)} %get-tuple-element.46), channel_id=1, source_target_pairs={{0,8},{8,0},{16,24},{24,16},{32,40},{40,32},{48,56},{56,48},{64,72... | collective-permute-start | bytes 24584 | tf_op jit(solution)/shard_map/ppermute | solution.py:165
  11.3 5.0 %collective-permute-start.3 = (f32[32,128]{0,1:T(8,128)S(1)}, f32[32,128]{0,1:T(8,128)S(1)}, u32[]{:S(2)}, u32[]{:S(2)}) collective-permute-start(f32[32,128]{0,1:T(8,128)S(1)} %broadcast_select_fusion), channel_id=1, source_target_pairs={{0,192},{8,200},{16,208},{24,216},{32,224},{40,232},{48,240},{56,2... | collective-permute-start | bytes 49160 | tf_op jit(solution)/shard_map/ppermute | solution.py:165
  26.3 5.0 %collective-permute-start.12 = (f32[128,128]{1,0:T(8,128)S(1)}, f32[128,128]{1,0:T(8,128)S(1)}, u32[]{:S(2)}, u32[]{:S(2)}) collective-permute-start(f32[128,128]{1,0:T(8,128)S(1)} %get-tuple-element.18), channel_id=1, source_target_pairs={{0,48},{8,56},{16,32},{24,40},{32,16},{40,24},{48,0},{56,8},{64,11... | collective-permute-start | bytes 196616 | tf_op jit(solution)/shard_map/ppermute | solution.py:165
  26.9 5.0 %collective-permute-start.10 = (f32[128,128]{1,0:T(8,128)S(1)}, f32[128,128]{1,0:T(8,128)S(1)}, u32[]{:S(2)}, u32[]{:S(2)}) collective-permute-start(f32[128,128]{1,0:T(8,128)S(1)} %get-tuple-element.16), channel_id=1, source_target_pairs={{0,16},{8,24},{16,0},{24,8},{32,48},{40,56},{48,32},{56,40},{64,80... | collective-permute-start | bytes 196616 | tf_op jit(solution)/shard_map/ppermute | solution.py:165
  31.9 5.1 %collective-permute-start.15 = (f32[128,128]{1,0:T(8,128)S(1)}, f32[128,128]{1,0:T(8,128)S(1)}, u32[]{:S(2)}, u32[]{:S(2)}) collective-permute-start(f32[128,128]{1,0:T(8,128)S(1)} %add_add_fusion), channel_id=1, source_target_pairs={{0,192},{8,200},{16,208},{24,216},{32,224},{40,232},{48,240},{56,2... | collective-permute-start | bytes 196616 | tf_op jit(solution)/shard_map/ppermute | solution.py:165
  32.8 4.9 %collective-permute-start.14 = (f32[128,128]{1,0:T(8,128)S(1)}, f32[128,128]{1,0:T(8,128)S(1)}, u32[]{:S(2)}, u32[]{:S(2)}) collective-permute-start(f32[128,128]{1,0:T(8,128)S(1)} %add_add_fusion), channel_id=1, source_target_pairs={{0,128},{8,136},{16,144},{24,152},{32,160},{40,168},{48,176},{56,1... | collective-permute-start | bytes 196616 | tf_op jit(solution)/shard_map/ppermute | solution.py:165
  38.3 7.2 %collective-permute-start.19 = (f32[32,128]{1,0:T(8,128)S(1)}, f32[32,128]{1,0:T(8,128)S(1)}, u32[]{:S(2)}, u32[]{:S(2)}) collective-permute-start(f32[32,128]{1,0:T(8,128)S(1)} %constant_dynamic-slice_fusion.3), channel_id=1, source_target_pairs={{0,8},{8,0},{16,24},{24,16},{32,40},{40,32},{48,56},{56,48},{64,72... | collective-permute-start | bytes 49160 | tf_op jit(solution)/shard_map/ppermute | solution.py:165
  48.8 6.9 %collective-permute-start.21 = (f32[4,32,128]{2,1,0:T(8,128)S(1)}, f32[4,32,128]{2,1,0:T(8,128)S(1)}, u32[]{:S(2)}, u32[]{:S(2)}) collective-permute-start(f32[4,32,128]{2,1,0:T(8,128)S(1)} %fusion.17), channel_id=1, source_target_pairs={{0,3},{1,2},{2,1},{3,0},{4,7},{5,6},{6,5},{7,4},{8,11},{9,10},{10,... | collective-permute-start | bytes 196616 | tf_op jit(solution)/shard_map/ppermute | solution.py:168
  51.9 9.0 %collective-permute-start.16 = (f32[128,128]{1,0:T(8,128)S(1)}, f32[128,128]{1,0:T(8,128)S(1)}, u32[]{:S(2)}, u32[]{:S(2)}) collective-permute-start(f32[128,128]{1,0:T(8,128)S(1)} %multiply_add_fusion.3.j0), channel_id=1, source_target_pairs={{0,16},{8,24},{16,0},{24,8},{32,48},{40,56},{48,32},{56,40},{64,80... | collective-permute-start | bytes 196616 | tf_op jit(solution)/shard_map/ppermute | solution.py:165
  52.9 8.0 %collective-permute-start.17 = (f32[128,128]{1,0:T(8,128)S(1)}, f32[128,128]{1,0:T(8,128)S(1)}, u32[]{:S(2)}, u32[]{:S(2)}) collective-permute-start(f32[128,128]{1,0:T(8,128)S(1)} %multiply_add_fusion.3.j0), channel_id=1, source_target_pairs={{0,32},{8,40},{16,48},{24,56},{32,0},{40,8},{48,16},{56,24},{64,96... | collective-permute-start | bytes 196616 | tf_op jit(solution)/shard_map/ppermute | solution.py:165
  54.7 6.1 %collective-permute-start.18 = (f32[128,128]{1,0:T(8,128)S(1)}, f32[128,128]{1,0:T(8,128)S(1)}, u32[]{:S(2)}, u32[]{:S(2)}) collective-permute-start(f32[128,128]{1,0:T(8,128)S(1)} %multiply_add_fusion.3.j0), channel_id=1, source_target_pairs={{0,48},{8,56},{16,32},{24,40},{32,16},{40,24},{48,0},{56,8},{64,11... | collective-permute-start | bytes 196616 | tf_op jit(solution)/shard_map/ppermute | solution.py:165
  55.8 9.7 %collective-permute-start.22 = (f32[32,128]{1,0:T(8,128)S(1)}, f32[32,128]{1,0:T(8,128)S(1)}, u32[]{:S(2)}, u32[]{:S(2)}) collective-permute-start(f32[32,128]{1,0:T(8,128)S(1)} %get-tuple-element.30), channel_id=1, source_target_pairs={{0,4},{1,5},{2,6},{3,7},{4,0},{5,1},{6,2},{7,3},{8,12},{9,13},{10,... | collective-permute-start | bytes 49160 | tf_op jit(solution)/shard_map/ppermute | solution.py:168
  68.7 5.0 %collective-permute-start.28 = (f32[128,128]{1,0:T(8,128)S(1)}, f32[128,128]{1,0:T(8,128)S(1)}, u32[]{:S(2)}, u32[]{:S(2)}) collective-permute-start(f32[128,128]{1,0:T(8,128)S(1)} %fusion.4), channel_id=1, source_target_pairs={{0,192},{8,200},{16,208},{24,216},{32,224},{40,232},{48,240},{56,2... | collective-permute-start | bytes 196616 | tf_op jit(solution)/shard_map/ppermute | solution.py:165
  75.2 6.4 %collective-permute-start.32 = (f32[32,128]{1,0:T(8,128)S(1)}, f32[32,128]{1,0:T(8,128)S(1)}, u32[]{:S(2)}, u32[]{:S(2)}) collective-permute-start(f32[32,128]{1,0:T(8,128)S(1)} %dynamic-slice_add_fusion), channel_id=1, source_target_pairs={{0,8},{8,0},{16,24},{24,16},{32,40},{40,32},{48,56},{56,48},{64,72... | collective-permute-start | bytes 49160 | tf_op jit(solution)/shard_map/ppermute | solution.py:165
  85.5 7.0 %collective-permute-start.29 = (f32[128,128]{1,0:T(8,128)S(1)}, f32[128,128]{1,0:T(8,128)S(1)}, u32[]{:S(2)}, u32[]{:S(2)}) collective-permute-start(f32[128,128]{1,0:T(8,128)S(1)} %multiply_add_fusion.1.j0), channel_id=1, source_target_pairs={{0,16},{8,24},{16,0},{24,8},{32,48},{40,56},{48,32},{56,40},{64,80... | collective-permute-start | bytes 196616 | tf_op jit(solution)/shard_map/ppermute | solution.py:165
  85.8 6.7 %collective-permute-start.30 = (f32[128,128]{1,0:T(8,128)S(1)}, f32[128,128]{1,0:T(8,128)S(1)}, u32[]{:S(2)}, u32[]{:S(2)}) collective-permute-start(f32[128,128]{1,0:T(8,128)S(1)} %multiply_add_fusion.1.j0), channel_id=1, source_target_pairs={{0,32},{8,40},{16,48},{24,56},{32,0},{40,8},{48,16},{56,24},{64,96... | collective-permute-start | bytes 196616 | tf_op jit(solution)/shard_map/ppermute | solution.py:165
  87.7 4.9 %collective-permute-start.31 = (f32[128,128]{1,0:T(8,128)S(1)}, f32[128,128]{1,0:T(8,128)S(1)}, u32[]{:S(2)}, u32[]{:S(2)}) collective-permute-start(f32[128,128]{1,0:T(8,128)S(1)} %multiply_add_fusion.1.j0), channel_id=1, source_target_pairs={{0,48},{8,56},{16,32},{24,40},{32,16},{40,24},{48,0},{56,8},{64,11... | collective-permute-start | bytes 196616 | tf_op jit(solution)/shard_map/ppermute | solution.py:165
  89.5 7.6 %collective-permute-start.35 = (f32[32,128]{1,0:T(8,128)S(1)}, f32[32,128]{1,0:T(8,128)S(1)}, u32[]{:S(2)}, u32[]{:S(2)}) collective-permute-start(f32[32,128]{1,0:T(8,128)S(1)} %get-tuple-element.28), channel_id=1, source_target_pairs={{0,4},{1,5},{2,6},{3,7},{4,0},{5,1},{6,2},{7,3},{8,12},{9,13},{10,... | collective-permute-start | bytes 49160 | tf_op jit(solution)/shard_map/ppermute | solution.py:168
  100.4 8.8 %collective-permute-start.41 = (f32[32,128]{0,1:T(8,128)S(1)}, f32[32,128]{0,1:T(8,128)S(1)}, u32[]{:S(2)}, u32[]{:S(2)}) collective-permute-start(f32[32,128]{0,1:T(8,128)S(1)} %get-tuple-element.41), channel_id=1, source_target_pairs={{0,192},{8,200},{16,208},{24,216},{32,224},{40,232},{48,240},{56,2... | collective-permute-start | bytes 49160 | tf_op jit(solution)/shard_map/ppermute | solution.py:165
  102.1 7.1 %collective-permute-start.40 = (f32[32,128]{0,1:T(8,128)S(1)}, f32[32,128]{0,1:T(8,128)S(1)}, u32[]{:S(2)}, u32[]{:S(2)}) collective-permute-start(f32[32,128]{0,1:T(8,128)S(1)} %get-tuple-element.42), channel_id=1, source_target_pairs={{0,128},{8,136},{16,144},{24,152},{32,160},{40,168},{48,176},{56,1... | collective-permute-start | bytes 49160 | tf_op jit(solution)/shard_map/ppermute | solution.py:165
  102.5 6.7 %collective-permute-start.39 = (f32[32,128]{0,1:T(8,128)S(1)}, f32[32,128]{0,1:T(8,128)S(1)}, u32[]{:S(2)}, u32[]{:S(2)}) collective-permute-start(f32[32,128]{0,1:T(8,128)S(1)} %get-tuple-element.40), channel_id=1, source_target_pairs={{0,64},{8,72},{16,80},{24,88},{32,96},{40,104},{48,112},{56,120},{... | collective-permute-start | bytes 49160 | tf_op jit(solution)/shard_map/ppermute | solution.py:165
  104.0 8.7 %collective-permute-start.43 = (f32[8,256]{1,0:T(8,128)S(1)}, f32[8,256]{1,0:T(8,128)S(1)}, u32[]{:S(2)}, u32[]{:S(2)}) collective-permute-start(f32[8,256]{1,0:T(8,128)S(1)} %get-tuple-element.44), channel_id=1, source_target_pairs={{0,8},{8,0},{16,24},{24,16},{32,40},{40,32},{48,56},{56,48},{64,72... | collective-permute-start | bytes 24584 | tf_op jit(solution)/shard_map/ppermute | solution.py:165
  (25 other events, 90.9 us)

commit v2 on v1

--- a/solution.py
+++ b/solution.py
@@ -24,6 +24,18 @@
         vector = vector / np.sqrt(np.sum(vector * vector))
         columns.append(vector.astype(np.float32))
     return np.stack(columns, axis=1)
+
+
+def fit_table(basis, sub_dev, band_count):
+    project = basis @ basis.T
+    table = np.zeros((sub_dev * band_count, 16), np.float32)
+    for band in range(band_count):
+        for core in range(sub_dev):
+            for to in range(4):
+                target = 2 * (band ^ to) + core
+                sources = [2 * band + core, 2 * (band ^ 4) + core, 2 * band + (core ^ 1), 2 * (band ^ 4) + (core ^ 1)]
+                table[2 * band + core, to::4] = project[target, sources]
+    return table
 
 
 def split(parts):
@@ -155,7 +167,6 @@
     penalty = penalty_gain * baseline_count / station_number
     basis = fit_basis(sub_dev * band_count)
     rows = 8 * dirs
-    share = rows // 4
 
     me = lax.axis_index("base")
     core, x, z = me & 1, (me >> 1) & 3, me >> 3
@@ -179,15 +190,23 @@
     def theirs_of(value):
         return jnp.where(core == 0, value[1], value[0])
 
+    plane_groups = [[8 * a + 2 * b + c for a in range(4) for b in range(4)] for c in range(2)]
+
+    def exchange(value):
+        return lax.all_to_all(value, "base", 0, 0, axis_index_groups=plane_groups, tiled=True)
+
+    def reorder(quarters):
+        quarters = [jnp.where(x & 1 == 0, quarters[a], quarters[a ^ 1]) for a in range(4)]
+        return [jnp.where(x & 2 == 0, quarters[a], quarters[a ^ 2]) for a in range(4)]
+
     turned = jones_deviation.transpose(0, 3, 2, 1).reshape(sub_dev, own_stations, rows)
-    identity = jnp.repeat(jnp.array([1.0, 0, 0, 0, 0, 0, 1.0, 0], jnp.float32), dirs)
-    turned = turned + identity
     mine, theirs = mine_of(turned), base_swap(theirs_of(turned), 1)
     chip = jnp.where(core == 0, jnp.concatenate([mine, theirs]), jnp.concatenate([theirs, mine]))
-    planes = [chip] + along_z([chip] * 3)
-    ordered = [jnp.where(z & 1 == 0, planes[a], planes[a ^ 1]) for a in range(4)]
-    ordered = [jnp.where(z & 2 == 0, ordered[a], ordered[a ^ 2]) for a in range(4)]
-    jones = jnp.concatenate(ordered).T
+    gathered = exchange(jnp.broadcast_to(chip, (16, *chip.shape)).reshape(-1, rows)).reshape(4, 4, 2 * own_stations, rows)
+    component = jnp.arange(rows)[:, None] // dirs
+    identity = jnp.where((component == 0) | (component == 6), 1.0, 0.0).astype(jnp.float32)
+    pieces = [q.reshape(LANES, rows).T + identity for q in reorder([gathered[:, a] for a in range(4)])]
+    jones = pieces[0]
 
     pairs = jnp.stack([antenna_first, antenna_second])
     pairs = jnp.concatenate([pairs, base_swap(pairs, 1)], axis=1)
@@ -198,45 +217,56 @@
     other_sky = base_swap(theirs_of(sky), 1)
     seen = jnp.concatenate([mine_of(observed), base_swap(theirs_of(observed), 1)], axis=1)
 
-    share_rows = jnp.arange(rows)[:, None] // share == z
     core_scalar = core.astype(jnp.int32).reshape(1)
-    own_basis = lax.dynamic_slice_in_dim(jnp.asarray(basis), 2 * band + core, 1, 0)[0]
-    next_basis = lax.dynamic_slice_in_dim(jnp.asarray(basis), 2 * band + 1 - core, 1, 0)[0]
-    far_basis = lax.dynamic_slice_in_dim(jnp.asarray(basis), 2 * (band ^ 4) + core, 1, 0)[0]
-
-    def fit(target):
-        beside = base_swap(target, 1)
-        partial = own_basis[:, None, None] * target + next_basis[:, None, None] * beside
-        for mask in (1, 3):
-            partial = partial + band_swap(partial, mask)
-        sent = band_swap(jnp.sum(far_basis[:, None, None] * partial, axis=0), 4)
-        return jnp.sum(own_basis[:, None, None] * partial, axis=0) + sent
-
-    dual = jnp.zeros((share, LANES), jnp.float32)
-    correction = None
+    table = fit_table(basis, sub_dev, band_count)
+    weights = lax.dynamic_slice_in_dim(jnp.asarray(table), 2 * band + core, 1, 0)[0].reshape(4, 4)
+    both_axes = ("base", "band")
+
+    across_z = [
+        (i * band_count + j, (i ^ 24) * band_count + (j ^ 4)) for i in range(base_count) for j in range(band_count)
+    ]
+
+    def after(value, *others):
+        return lax.optimization_barrier((value, *others))[0]
+
+    jones, weights = lax.optimization_barrier((jones, tuple(weights[k] for k in range(4))))
+    dual = jnp.zeros((rows, LANES), jnp.float32)
     residual = None
     for iteration in range(ITERS):
-        pieces = [jones] + along_x([jones] * 3)
+        if iteration:
+            pieces = [jones] + along_x([jones] * 3)
+            target = jones + dual / penalty
+            pair = jnp.stack([target, lax.ppermute(target, both_axes, across_z)])
+            pair = after(pair, *pieces[1:]) if True else pair
+            four = [*pair, *base_swap(pair, 1)]
+            meant = sum(weights[k][:, None, None] * four[k] for k in range(4))
         *terms, residual = iterate(core_scalar, pieces, sky, other_sky, seen, place, column)
-        received = along_x(terms[1:])
+        last_one = iteration + 1 == ITERS
+        received = None if last_one else along_x(terms[1:])
         if iteration:
-            held = lax.dynamic_slice_in_dim(jones, z * share, share, 0)
-            consensus = fit(held + dual / penalty)
-            dual = dual + penalty * (held - consensus)
-            correction = dual + penalty * (held - consensus)
-            spread = jnp.where(share_rows, jnp.concatenate([correction] * 4), 0.0)
-            summed = terms[0] - spread + received[0] + received[1] + received[2]
+            sent = meant[1:3]
+            if 1 == 1:
+                sent = after(sent, terms[0])
+            elif 1 == 2 and not last_one:
+                sent = after(sent, *received)
+            came = band_swap(sent, 1)
+            further = meant[3] + came[1]
+            if 0 == 1 and not last_one:
+                further = after(further, *received)
+            consensus = meant[0] + came[0] + band_swap(further, 3)
+            dual = dual + penalty * (jones - consensus)
+            jones_next = jones - step_size * (dual + penalty * (jones - consensus))
         else:
+            jones_next = jones
+        if not last_one:
             summed = terms[0] + received[0] + received[1] + received[2]
-        if iteration + 1 < ITERS:
             others = along_z([summed] * 3)
-            jones = jones + step_size * (summed + others[0] + others[1] + others[2])
+            jones = jones_next + step_size * (summed + others[0] + others[1] + others[2])
     per_station = 2 * own_stations
-    turned_sum = summed.T
-    parts = [lax.dynamic_slice_in_dim(turned_sum, (z ^ k) * per_station, per_station, 0) for k in range(4)]
-    others = along_z(parts[1:])
-    last = lax.dynamic_slice_in_dim(jones.T, z * per_station, per_station, 0)
-    last = last + step_size * (parts[0] + others[0] + others[1] + others[2])
+    leaving = jnp.stack([q.T.reshape(4, per_station, rows) for q in reorder(terms)], axis=1)
+    came = exchange(leaving.reshape(16 * per_station, rows)).reshape(16, per_station, rows)
+    last = lax.dynamic_slice_in_dim(jones_next.T, z * per_station, per_station, 0)
+    last = last + step_size * jnp.sum(came, axis=0)
     last = last.reshape(2, own_stations, rows)
     kept, given = mine_of(last), base_swap(theirs_of(last), 1)
     both = jnp.where(core == 0, jnp.stack([kept, given]), jnp.stack([given, kept]))

time: 115 us -> 107 us (0.930)
  starting transfers between devices: 73.6 us -> 60.1 us
  waiting for transfers between devices: 29.2 us -> 33.2 us
    ppermute x38 -> x26, starting transfers between devices: 60.4 us -> 36.7 us  [base_swap(): lax.ppermute(value, 'base', [(i, i ^ mask) for i in range(base_count)])]
    all_to_all x0 -> x2, waiting for transfers between devices: none -> 14.3 us  [exchange(): lax.all_to_all(value, 'base', 0, 0, axis_index_groups=plane_groups, tiled...]
    all_to_all x0 -> x2, starting transfers between devices: none -> 12.7 us  [exchange(): lax.all_to_all(value, 'base', 0, 0, axis_index_groups=plane_groups, tiled...]
    ppermute x38 -> x26, waiting for transfers between devices: 24.3 us -> 13.1 us  [base_swap(): lax.ppermute(value, 'base', [(i, i ^ mask) for i in range(base_count)])]
    ppermute x6 -> x4, starting transfers between devices: 13.2 us -> 7.39 us  [band_swap(): lax.ppermute(value, 'band', [(i, i ^ mask) for i in range(band_count)])]
    ppermute x0 -> x2, waiting for transfers between devices: none -> 4.82 us  [per_device(): pair = jnp.stack([target, lax.ppermute(target, both_axes, across_z)])]
    ppermute x6 -> x4, waiting for transfers between devices: 4.93 us -> 0.95 us  [band_swap(): lax.ppermute(value, 'band', [(i, i ^ mask) for i in range(band_count)])]
    ppermute x0 -> x2, starting transfers between devices: none -> 3.29 us  [per_device(): pair = jnp.stack([target, lax.ppermute(target, both_axes, across_z)])]
  transfers between devices with their start and end apart: 44 -> 34, of which waited for: 21 -> 15; matrix products, arithmetic and copies ran while one was open for 2% -> 6% of each run, Pallas kernels for 2% -> 2%
where the time goes in v2:
time: 107 us
  starting transfers between devices  60.1 us (56%)
  waiting for transfers between devices  33.2 us (31%)
  local copies, waits for them, and re-layouts  5.1 us (5%)
  Pallas kernels  4.02 us (4%)
  other arithmetic  3.07 us (3%)
  between operations  1.08 us (1%)
    ppermute x26, starting transfers between devices, base_swap(): lax.ppermute(value, 'base', [(i, i ^ mask) for i in range(base_count)])  36.7 us
    all_to_all x2, waiting for transfers between devices, exchange(): lax.all_to_all(value, 'base', 0, 0, axis_index_groups=plane_groups, tiled...  14.3 us
    ppermute x26, waiting for transfers between devices, base_swap(): lax.ppermute(value, 'base', [(i, i ^ mask) for i in range(base_count)])  13.1 us
    all_to_all x2, starting transfers between devices, exchange(): lax.all_to_all(value, 'base', 0, 0, axis_index_groups=plane_groups, tiled...  12.7 us
    ppermute x4, starting transfers between devices, band_swap(): lax.ppermute(value, 'band', [(i, i ^ mask) for i in range(band_count)])  7.39 us
    ppermute x2, waiting for transfers between devices, per_device(): pair = jnp.stack([target, lax.ppermute(target, both_axes, across_z)])  4.82 us
    pallas_call x3, Pallas kernels, iterate(): pl.pallas_call(functools.partial(iteration_kernel, dirs), out_shape=[piec...  4.02 us
    ppermute x2, starting transfers between devices, per_device(): pair = jnp.stack([target, lax.ppermute(target, both_axes, across_z)])  3.29 us
  transfers between devices with their start and end apart: 34, of which 15 were waited for; matrix products, arithmetic and copies ran while one was open for 6% of the time, Pallas kernels for 2%

profile of v2, /device:TPU:1, one launch (start us, length us, event | category | flops | bytes accessed | tf_op | source)
XLA Modules:
  0.0 106.6 jit_solution(17163791644835203767)
XLA Ops:
  1.3 3.3 %collective-permute-start.3 = (s32[2,256]{1,0:T(2,128)S(1)}, s32[2,256]{1,0:T(2,128)S(1)}, u32[]{:S(2)}, u32[]{:S(2)}) collective-permute-start(s32[2,256]{1,0:T(2,128)S(1)} %pad_add_fusion.1), channel_id=1, source_target_pairs={{0,8},{8,0},{16,24},{24,16},{32,40},{40,32},{48,56},{56,48},{64,72... | collective-permute-start | bytes 6152 | tf_op jit(solution)/shard_map/ppermute | solution.py:176
  7.7 6.6 %all-to-all-start = ((f32[16,32,128]{2,1,0:T(8,128)}), f32[16,32,128]{2,1,0:T(8,128)S(1)}, u32[]{:S(2)}, u32[]{:S(2)}) async-start(f32[16,32,128]{2,1,0:T(8,128)} %broadcast_in_dim.10), calls=%async_computation | async-start | bytes 524288 | tf_op jit(solution)/shard_map/all_to_all | solution.py:196
  15.3 9.0 %all-to-all-done = f32[16,32,128]{2,1,0:T(8,128)S(1)} async-done(((f32[16,32,128]{2,1,0:T(8,128)}), f32[16,32,128]{2,1,0:T(8,128)S(1)}, u32[]{:S(2)}, u32[]{:S(2)}) %all-to-all-start) | async-done | bytes 262176 | tf_op jit(solution)/shard_map/all_to_all | solution.py:196
  24.9 1.4 %shard_map.77 = (f32[128,128]{1,0:T(8,128)S(1)}, f32[128,128]{1,0:T(8,128)S(1)}, f32[128,128]{1,0:T(8,128)S(1)}, f32[128,128]{1,0:T(8,128)S(1)}, f32[8,512]{1,0:T(8,128)}) custom-call(s32[1]{0:T(128)} %bitcast.8.core_ref, f32[128,128]{1,0:T(8,128)S(1)} %get-tuple-element.24.j0, f32[128,128]{1,0:T(8,128)S(1)} %get-tuple-element.74.j1, ...), custom_call_target="tpu_custom_call" | custom-call | flops 536870912 | bytes 2097152 | tf_op jit(solution)/shard_map/pallas_call | solution.py:143
  26.7 3.5 %collective-permute-start.6 = (f32[128,128]{1,0:T(8,128)S(1)}, f32[128,128]{1,0:T(8,128)S(1)}, u32[]{:S(2)}, u32[]{:S(2)}) collective-permute-start(f32[128,128]{1,0:T(8,128)S(1)} %get-tuple-element.28), channel_id=1, source_target_pairs={{0,48},{8,56},{16,32},{24,40},{32,16},{40,24},{48,0},{56,8},{64,11... | collective-permute-start | bytes 196616 | tf_op jit(solution)/shard_map/ppermute | solution.py:176
  32.1 2.8 %collective-permute-start.9 = (f32[128,128]{1,0:T(8,128)S(1)}, f32[128,128]{1,0:T(8,128)S(1)}, u32[]{:S(2)}, u32[]{:S(2)}) collective-permute-start(f32[128,128]{1,0:T(8,128)S(1)} %add_add_fusion.2), channel_id=1, source_target_pairs={{0,192},{8,200},{16,208},{24,216},{32,224},{40,232},{48,240},{56,2... | collective-permute-start | bytes 196616 | tf_op jit(solution)/shard_map/ppermute | solution.py:176
  37.1 2.0 %collective-permute-done.8 = f32[128,128]{1,0:T(8,128)S(1)} collective-permute-done((f32[128,128]{1,0:T(8,128)S(1)}, f32[128,128]{1,0:T(8,128)S(1)}, u32[]{:S(2)}, u32[]{:S(2)}) %collective-permute-start.8) | collective-permute-done | bytes 65568 | tf_op jit(solution)/shard_map/ppermute | solution.py:176
  39.2 3.3 %collective-permute-start.10 = (f32[128,128]{1,0:T(8,128)S(1)}, f32[128,128]{1,0:T(8,128)S(1)}, u32[]{:S(2)}, u32[]{:S(2)}) collective-permute-start(f32[128,128]{1,0:T(8,128)S(1)} %multiply_add_fusion.3.j0), channel_id=1, source_target_pairs={{0,196},{1,197},{2,198},{3,199},{4,192},{5,193},{6,194},{7,195},{8... | collective-permute-start | bytes 196616 | tf_op jit(solution)/shard_map/ppermute | solution.py:239
  42.5 2.3 %collective-permute-start.13 = (f32[128,128]{1,0:T(8,128)S(1)}, f32[128,128]{1,0:T(8,128)S(1)}, u32[]{:S(2)}, u32[]{:S(2)}) collective-permute-start(f32[128,128]{1,0:T(8,128)S(1)} %multiply_add_fusion.3.j0), channel_id=1, source_target_pairs={{0,48},{8,56},{16,32},{24,40},{32,16},{40,24},{48,0},{56,8},{64,11... | collective-permute-start | bytes 196616 | tf_op jit(solution)/shard_map/ppermute | solution.py:176
  46.8 2.5 %collective-permute-done.12.j2 = f32[128,128]{1,0:T(8,128)S(1)} collective-permute-done((f32[128,128]{1,0:T(8,128)S(1)}, f32[128,128]{1,0:T(8,128)S(1)}, u32[]{:S(2)}, u32[]{:S(2)}) %collective-permute-start.12) | collective-permute-done | bytes 65568 | tf_op jit(solution)/shard_map/ppermute | solution.py:176
  49.4 4.9 %collective-permute-start.14 = (f32[2,128,128]{2,1,0:T(8,128)S(1)}, f32[2,128,128]{2,1,0:T(8,128)S(1)}, u32[]{:S(2)}, u32[]{:S(2)}) collective-permute-start(f32[2,128,128]{2,1,0:T(8,128)S(1)} %pad_maximum_fusion.1), channel_id=1, source_target_pairs={{0,8},{8,0},{16,24},{24,16},{32,40},{40,32},{48,56},{56,48},{64,72... | collective-permute-start | bytes 393224 | tf_op jit(solution)/shard_map/ppermute | solution.py:176
  54.3 1.4 %shard_map.78 = (f32[128,128]{1,0:T(8,128)S(1)}, f32[128,128]{1,0:T(8,128)S(1)}, f32[128,128]{1,0:T(8,128)S(1)}, f32[128,128]{1,0:T(8,128)S(1)}, f32[8,512]{1,0:T(8,128)}) custom-call(s32[1]{0:T(128)} %bitcast.8.core_ref, f32[128,128]{1,0:T(8,128)S(1)} %multiply_add_fusion.3.j0, f32[128,128]{1,0:T(8,128)S(1)} %collective-permute-done.11.j1, ...), custom_call_target="tpu_custom_call" | custom-call | flops 536870912 | bytes 2097152 | tf_op jit(solution)/shard_map/pallas_call | solution.py:143
  55.7 2.2 %collective-permute-start.18 = (f32[128,128]{1,0:T(8,128)S(1)}, f32[128,128]{1,0:T(8,128)S(1)}, u32[]{:S(2)}, u32[]{:S(2)}) collective-permute-start(f32[128,128]{1,0:T(8,128)S(1)} %get-tuple-element.37), channel_id=1, source_target_pairs={{0,32},{8,40},{16,48},{24,56},{32,0},{40,8},{48,16},{56,24},{64,96... | collective-permute-start | bytes 196616 | tf_op jit(solution)/shard_map/ppermute | solution.py:176
  57.9 1.7 %collective-permute-start.19 = (f32[128,128]{1,0:T(8,128)S(1)}, f32[128,128]{1,0:T(8,128)S(1)}, u32[]{:S(2)}, u32[]{:S(2)}) collective-permute-start(f32[128,128]{1,0:T(8,128)S(1)} %get-tuple-element.38), channel_id=1, source_target_pairs={{0,48},{8,56},{16,32},{24,40},{32,16},{40,24},{48,0},{56,8},{64,11... | collective-permute-start | bytes 196616 | tf_op jit(solution)/shard_map/ppermute | solution.py:176
  62.3 2.5 %collective-permute-start.22 = (f32[128,128]{1,0:T(8,128)S(1)}, f32[128,128]{1,0:T(8,128)S(1)}, u32[]{:S(2)}, u32[]{:S(2)}) collective-permute-start(f32[128,128]{1,0:T(8,128)S(1)} %add_add_fusion.1), channel_id=1, source_target_pairs={{0,192},{8,200},{16,208},{24,216},{32,224},{40,232},{48,240},{56,2... | collective-permute-start | bytes 196616 | tf_op jit(solution)/shard_map/ppermute | solution.py:176
  66.0 2.8 %collective-permute-start.16 = (f32[128,128]{1,0:T(8,128)S(1)}, f32[128,128]{1,0:T(8,128)S(1)}, u32[]{:S(2)}, u32[]{:S(2)}) collective-permute-start(f32[128,128]{1,0:T(8,128)S(1)} %fusion.9), channel_id=1, source_target_pairs={{0,3},{1,2},{2,1},{3,0},{4,7},{5,6},{6,5},{7,4},{8,11},{9,10},{10,... | collective-permute-start | bytes 196616 | tf_op jit(solution)/shard_map/ppermute | solution.py:179
  68.8 3.1 %collective-permute-done.21 = f32[128,128]{1,0:T(8,128)S(1)} collective-permute-done((f32[128,128]{1,0:T(8,128)S(1)}, f32[128,128]{1,0:T(8,128)S(1)}, u32[]{:S(2)}, u32[]{:S(2)}) %collective-permute-start.21) | collective-permute-done | bytes 65568 | tf_op jit(solution)/shard_map/ppermute | solution.py:176
  72.0 1.8 %collective-permute-start.26 = (f32[128,128]{1,0:T(8,128)S(1)}, f32[128,128]{1,0:T(8,128)S(1)}, u32[]{:S(2)}, u32[]{:S(2)}) collective-permute-start(f32[128,128]{1,0:T(8,128)S(1)} %get-tuple-element.47.j0), channel_id=1, source_target_pairs={{0,48},{8,56},{16,32},{24,40},{32,16},{40,24},{48,0},{56,8},{64,11... | collective-permute-start | bytes 196616 | tf_op jit(solution)/shard_map/ppermute | solution.py:176
  75.4 4.8 %collective-permute-done.23 = f32[128,128]{1,0:T(8,128)S(1)} collective-permute-done((f32[128,128]{1,0:T(8,128)S(1)}, f32[128,128]{1,0:T(8,128)S(1)}, u32[]{:S(2)}, u32[]{:S(2)}) %collective-permute-start.23) | collective-permute-done | bytes 65568 | tf_op jit(solution)/shard_map/ppermute | solution.py:239
  80.2 3.6 %collective-permute-start.27 = (f32[2,128,128]{2,1,0:T(8,128)S(1)}, f32[2,128,128]{2,1,0:T(8,128)S(1)}, u32[]{:S(2)}, u32[]{:S(2)}) collective-permute-start(f32[2,128,128]{2,1,0:T(8,128)S(1)} %pad_maximum_fusion.2), channel_id=1, source_target_pairs={{0,8},{8,0},{16,24},{24,16},{32,40},{40,32},{48,56},{56,48},{64,72... | collective-permute-start | bytes 393224 | tf_op jit(solution)/shard_map/ppermute | solution.py:176
  86.8 6.1 %all-to-all-start.1 = ((f32[16,32,128]{2,1,0:T(8,128)}), f32[16,32,128]{2,1,0:T(8,128)S(1)}, u32[]{:S(2)}, u32[]{:S(2)}) async-start(f32[16,32,128]{2,1,0:T(8,128)} %bitcast.47), calls=%async_computation.1 | async-start | bytes 524288 | tf_op jit(solution)/shard_map/all_to_all | solution.py:196
  92.9 2.8 %collective-permute-start.29 = (f32[128,128]{1,0:T(8,128)S(1)}, f32[128,128]{1,0:T(8,128)S(1)}, u32[]{:S(2)}, u32[]{:S(2)}) collective-permute-start(f32[128,128]{1,0:T(8,128)S(1)} %fusion.6), channel_id=1, source_target_pairs={{0,3},{1,2},{2,1},{3,0},{4,7},{5,6},{6,5},{7,4},{8,11},{9,10},{10,... | collective-permute-start | bytes 196616 | tf_op jit(solution)/shard_map/ppermute | solution.py:179
  97.4 5.3 %all-to-all-done.1 = f32[16,32,128]{2,1,0:T(8,128)S(1)} async-done(((f32[16,32,128]{2,1,0:T(8,128)}), f32[16,32,128]{2,1,0:T(8,128)S(1)}, u32[]{:S(2)}, u32[]{:S(2)}) %all-to-all-start.1) | async-done | bytes 262176 | tf_op jit(solution)/shard_map/all_to_all | solution.py:196
  103.0 2.0 %collective-permute-start.30 = (f32[16,128]{0,1:T(8,128)S(1)}, f32[16,128]{0,1:T(8,128)S(1)}, u32[]{:S(2)}, u32[]{:S(2)}) collective-permute-start(f32[16,128]{0,1:T(8,128)S(1)} %get-tuple-element.68), channel_id=1, source_target_pairs={{0,8},{8,0},{16,24},{24,16},{32,40},{40,32},{48,56},{56,48},{64,72... | collective-permute-start | bytes 24584 | tf_op jit(solution)/shard_map/ppermute | solution.py:176
  (115 shorter events, 23.7 us)
Async XLA Ops:
  1.3 13.7 %collective-permute-start.3 = (s32[2,256]{1,0:T(2,128)S(1)}, s32[2,256]{1,0:T(2,128)S(1)}, u32[]{:S(2)}, u32[]{:S(2)}) collective-permute-start(s32[2,256]{1,0:T(2,128)S(1)} %pad_add_fusion.1), channel_id=1, source_target_pairs={{0,8},{8,0},{16,24},{24,16},{32,40},{40,32},{48,56},{56,48},{64,72... | collective-permute-start | bytes 6152 | tf_op jit(solution)/shard_map/ppermute | solution.py:176
  6.4 8.9 %collective-permute-start.2 = (f32[8,256]{1,0:T(8,128)S(1)}, f32[8,256]{1,0:T(8,128)S(1)}, u32[]{:S(2)}, u32[]{:S(2)}) collective-permute-start(f32[8,256]{1,0:T(8,128)S(1)} %get-tuple-element.72), channel_id=1, source_target_pairs={{0,8},{8,0},{16,24},{24,16},{32,40},{40,32},{48,56},{56,48},{64,72... | collective-permute-start | bytes 24584 | tf_op jit(solution)/shard_map/ppermute | solution.py:176
  7.7 16.7 %all-to-all-start = ((f32[16,32,128]{2,1,0:T(8,128)}), f32[16,32,128]{2,1,0:T(8,128)S(1)}, u32[]{:S(2)}, u32[]{:S(2)}) async-start(f32[16,32,128]{2,1,0:T(8,128)} %broadcast_in_dim.10), calls=%async_computation | async-start | bytes 524288 | tf_op jit(solution)/shard_map/all_to_all | solution.py:196
  14.4 10.5 %collective-permute-start.1 = (f32[128,256]{1,0:T(8,128)S(1)}, f32[128,256]{1,0:T(8,128)S(1)}, u32[]{:S(2)}, u32[]{:S(2)}) collective-permute-start(f32[128,256]{1,0:T(8,128)S(1)} %bitcast.121), channel_id=1, source_target_pairs={{0,8},{8,0},{16,24},{24,16},{32,40},{40,32},{48,56},{56,48},{64,72... | collective-permute-start | bytes 393224 | tf_op jit(solution)/shard_map/ppermute | solution.py:176
  26.7 5.0 %collective-permute-start.5 = (f32[128,128]{1,0:T(8,128)S(1)}, f32[128,128]{1,0:T(8,128)S(1)}, u32[]{:S(2)}, u32[]{:S(2)}) collective-permute-start(f32[128,128]{1,0:T(8,128)S(1)} %get-tuple-element.27), channel_id=1, source_target_pairs={{0,32},{8,40},{16,48},{24,56},{32,0},{40,8},{48,16},{56,24},{64,96... | collective-permute-start | bytes 196616 | tf_op jit(solution)/shard_map/ppermute | solution.py:176
  26.7 5.5 %collective-permute-start.6 = (f32[128,128]{1,0:T(8,128)S(1)}, f32[128,128]{1,0:T(8,128)S(1)}, u32[]{:S(2)}, u32[]{:S(2)}) collective-permute-start(f32[128,128]{1,0:T(8,128)S(1)} %get-tuple-element.28), channel_id=1, source_target_pairs={{0,48},{8,56},{16,32},{24,40},{32,16},{40,24},{48,0},{56,8},{64,11... | collective-permute-start | bytes 196616 | tf_op jit(solution)/shard_map/ppermute | solution.py:176
  32.1 5.0 %collective-permute-start.9 = (f32[128,128]{1,0:T(8,128)S(1)}, f32[128,128]{1,0:T(8,128)S(1)}, u32[]{:S(2)}, u32[]{:S(2)}) collective-permute-start(f32[128,128]{1,0:T(8,128)S(1)} %add_add_fusion.2), channel_id=1, source_target_pairs={{0,192},{8,200},{16,208},{24,216},{32,224},{40,232},{48,240},{56,2... | collective-permute-start | bytes 196616 | tf_op jit(solution)/shard_map/ppermute | solution.py:176
  39.2 6.5 %collective-permute-start.10 = (f32[128,128]{1,0:T(8,128)S(1)}, f32[128,128]{1,0:T(8,128)S(1)}, u32[]{:S(2)}, u32[]{:S(2)}) collective-permute-start(f32[128,128]{1,0:T(8,128)S(1)} %multiply_add_fusion.3.j0), channel_id=1, source_target_pairs={{0,196},{1,197},{2,198},{3,199},{4,192},{5,193},{6,194},{7,195},{8... | collective-permute-start | bytes 196616 | tf_op jit(solution)/shard_map/ppermute | solution.py:239
  49.4 10.2 %collective-permute-start.14 = (f32[2,128,128]{2,1,0:T(8,128)S(1)}, f32[2,128,128]{2,1,0:T(8,128)S(1)}, u32[]{:S(2)}, u32[]{:S(2)}) collective-permute-start(f32[2,128,128]{2,1,0:T(8,128)S(1)} %pad_maximum_fusion.1), channel_id=1, source_target_pairs={{0,8},{8,0},{16,24},{24,16},{32,40},{40,32},{48,56},{56,48},{64,72... | collective-permute-start | bytes 393224 | tf_op jit(solution)/shard_map/ppermute | solution.py:176
  55.7 5.5 %collective-permute-start.17 = (f32[128,128]{1,0:T(8,128)S(1)}, f32[128,128]{1,0:T(8,128)S(1)}, u32[]{:S(2)}, u32[]{:S(2)}) collective-permute-start(f32[128,128]{1,0:T(8,128)S(1)} %get-tuple-element.36), channel_id=1, source_target_pairs={{0,16},{8,24},{16,0},{24,8},{32,48},{40,56},{48,32},{56,40},{64,80... | collective-permute-start | bytes 196616 | tf_op jit(solution)/shard_map/ppermute | solution.py:176
  55.7 5.8 %collective-permute-start.18 = (f32[128,128]{1,0:T(8,128)S(1)}, f32[128,128]{1,0:T(8,128)S(1)}, u32[]{:S(2)}, u32[]{:S(2)}) collective-permute-start(f32[128,128]{1,0:T(8,128)S(1)} %get-tuple-element.37), channel_id=1, source_target_pairs={{0,32},{8,40},{16,48},{24,56},{32,0},{40,8},{48,16},{56,24},{64,96... | collective-permute-start | bytes 196616 | tf_op jit(solution)/shard_map/ppermute | solution.py:176
  59.8 6.2 %collective-permute-start.15 = (f32[2,128,128]{2,1,0:T(8,128)S(1)}, f32[2,128,128]{2,1,0:T(8,128)S(1)}, u32[]{:S(2)}, u32[]{:S(2)}) collective-permute-start(f32[2,128,128]{2,1,0:T(8,128)S(1)} %slice.137), channel_id=1, source_target_pairs={{0,1},{1,0},{2,3},{3,2},{4,5},{5,4},{6,7},{7,6},{8,9},{9,8},{10,11... | collective-permute-start | bytes 393224 | tf_op jit(solution)/shard_map/ppermute | solution.py:179
  62.3 6.5 %collective-permute-start.22 = (f32[128,128]{1,0:T(8,128)S(1)}, f32[128,128]{1,0:T(8,128)S(1)}, u32[]{:S(2)}, u32[]{:S(2)}) collective-permute-start(f32[128,128]{1,0:T(8,128)S(1)} %add_add_fusion.1), channel_id=1, source_target_pairs={{0,192},{8,200},{16,208},{24,216},{32,224},{40,232},{48,240},{56,2... | collective-permute-start | bytes 196616 | tf_op jit(solution)/shard_map/ppermute | solution.py:176
  64.8 7.1 %collective-permute-start.21 = (f32[128,128]{1,0:T(8,128)S(1)}, f32[128,128]{1,0:T(8,128)S(1)}, u32[]{:S(2)}, u32[]{:S(2)}) collective-permute-start(f32[128,128]{1,0:T(8,128)S(1)} %add_add_fusion.1), channel_id=1, source_target_pairs={{0,128},{8,136},{16,144},{24,152},{32,160},{40,168},{48,176},{56,1... | collective-permute-start | bytes 196616 | tf_op jit(solution)/shard_map/ppermute | solution.py:176
  65.2 6.8 %collective-permute-start.20 = (f32[128,128]{1,0:T(8,128)S(1)}, f32[128,128]{1,0:T(8,128)S(1)}, u32[]{:S(2)}, u32[]{:S(2)}) collective-permute-start(f32[128,128]{1,0:T(8,128)S(1)} %add_add_fusion.1), channel_id=1, source_target_pairs={{0,64},{8,72},{16,80},{24,88},{32,96},{40,104},{48,112},{56,120},{... | collective-permute-start | bytes 196616 | tf_op jit(solution)/shard_map/ppermute | solution.py:176
  66.0 6.0 %collective-permute-start.16 = (f32[128,128]{1,0:T(8,128)S(1)}, f32[128,128]{1,0:T(8,128)S(1)}, u32[]{:S(2)}, u32[]{:S(2)}) collective-permute-start(f32[128,128]{1,0:T(8,128)S(1)} %fusion.9), channel_id=1, source_target_pairs={{0,3},{1,2},{2,1},{3,0},{4,7},{5,6},{6,5},{7,4},{8,11},{9,10},{10,... | collective-permute-start | bytes 196616 | tf_op jit(solution)/shard_map/ppermute | solution.py:179
  72.0 8.2 %collective-permute-start.26 = (f32[128,128]{1,0:T(8,128)S(1)}, f32[128,128]{1,0:T(8,128)S(1)}, u32[]{:S(2)}, u32[]{:S(2)}) collective-permute-start(f32[128,128]{1,0:T(8,128)S(1)} %get-tuple-element.47.j0), channel_id=1, source_target_pairs={{0,48},{8,56},{16,32},{24,40},{32,16},{40,24},{48,0},{56,8},{64,11... | collective-permute-start | bytes 196616 | tf_op jit(solution)/shard_map/ppermute | solution.py:176
  73.8 6.4 %collective-permute-start.25 = (f32[128,128]{1,0:T(8,128)S(1)}, f32[128,128]{1,0:T(8,128)S(1)}, u32[]{:S(2)}, u32[]{:S(2)}) collective-permute-start(f32[128,128]{1,0:T(8,128)S(1)} %get-tuple-element.47.j0), channel_id=1, source_target_pairs={{0,32},{8,40},{16,48},{24,56},{32,0},{40,8},{48,16},{56,24},{64,96... | collective-permute-start | bytes 196616 | tf_op jit(solution)/shard_map/ppermute | solution.py:176
  74.8 5.4 %collective-permute-start.24 = (f32[128,128]{1,0:T(8,128)S(1)}, f32[128,128]{1,0:T(8,128)S(1)}, u32[]{:S(2)}, u32[]{:S(2)}) collective-permute-start(f32[128,128]{1,0:T(8,128)S(1)} %get-tuple-element.47.j0), channel_id=1, source_target_pairs={{0,16},{8,24},{16,0},{24,8},{32,48},{40,56},{48,32},{56,40},{64,80... | collective-permute-start | bytes 196616 | tf_op jit(solution)/shard_map/ppermute | solution.py:176
  75.3 4.8 %collective-permute-start.23 = (f32[128,128]{1,0:T(8,128)S(1)}, f32[128,128]{1,0:T(8,128)S(1)}, u32[]{:S(2)}, u32[]{:S(2)}) collective-permute-start(f32[128,128]{1,0:T(8,128)S(1)} %get-tuple-element.46), channel_id=1, source_target_pairs={{0,196},{1,197},{2,198},{3,199},{4,192},{5,193},{6,194},{7,195},{8... | collective-permute-start | bytes 196616 | tf_op jit(solution)/shard_map/ppermute | solution.py:239
  80.2 4.8 %collective-permute-start.27 = (f32[2,128,128]{2,1,0:T(8,128)S(1)}, f32[2,128,128]{2,1,0:T(8,128)S(1)}, u32[]{:S(2)}, u32[]{:S(2)}) collective-permute-start(f32[2,128,128]{2,1,0:T(8,128)S(1)} %pad_maximum_fusion.2), channel_id=1, source_target_pairs={{0,8},{8,0},{16,24},{24,16},{32,40},{40,32},{48,56},{56,48},{64,72... | collective-permute-start | bytes 393224 | tf_op jit(solution)/shard_map/ppermute | solution.py:176
  85.2 7.7 %collective-permute-start.28 = (f32[2,128,128]{2,1,0:T(8,128)S(1)}, f32[2,128,128]{2,1,0:T(8,128)S(1)}, u32[]{:S(2)}, u32[]{:S(2)}) collective-permute-start(f32[2,128,128]{2,1,0:T(8,128)S(1)} %slice.142), channel_id=1, source_target_pairs={{0,1},{1,0},{2,3},{3,2},{4,5},{5,4},{6,7},{7,6},{8,9},{9,8},{10,11... | collective-permute-start | bytes 393224 | tf_op jit(solution)/shard_map/ppermute | solution.py:179
  86.8 15.8 %all-to-all-start.1 = ((f32[16,32,128]{2,1,0:T(8,128)}), f32[16,32,128]{2,1,0:T(8,128)S(1)}, u32[]{:S(2)}, u32[]{:S(2)}) async-start(f32[16,32,128]{2,1,0:T(8,128)} %bitcast.47), calls=%async_computation.1 | async-start | bytes 524288 | tf_op jit(solution)/shard_map/all_to_all | solution.py:196
  95.7 9.3 %collective-permute-start.31 = (f32[8,256]{1,0:T(8,128)S(1)}, f32[8,256]{1,0:T(8,128)S(1)}, u32[]{:S(2)}, u32[]{:S(2)}) collective-permute-start(f32[8,256]{1,0:T(8,128)S(1)} %get-tuple-element.70), channel_id=1, source_target_pairs={{0,8},{8,0},{16,24},{24,16},{32,40},{40,32},{48,56},{56,48},{64,72... | collective-permute-start | bytes 24584 | tf_op jit(solution)/shard_map/ppermute | solution.py:176
  (14 other events, 48.2 us)

commit v3 on v2

--- a/solution.py
+++ b/solution.py
@@ -208,6 +208,9 @@
     pieces = [q.reshape(LANES, rows).T + identity for q in reorder([gathered[:, a] for a in range(4)])]
     jones = pieces[0]
 
+    antenna_first, antenna_second, coherency, observed = lax.optimization_barrier(
+        (antenna_first, antenna_second, coherency, observed, theirs)
+    )[:4]
     pairs = jnp.stack([antenna_first, antenna_second])
     pairs = jnp.concatenate([pairs, base_swap(pairs, 1)], axis=1)
     place = ((((pairs >> 5) & 3) ^ x) << 7) | ((pairs >> 7) << 5) | (pairs & 31)
@@ -237,42 +240,39 @@
             pieces = [jones] + along_x([jones] * 3)
             target = jones + dual / penalty
             pair = jnp.stack([target, lax.ppermute(target, both_axes, across_z)])
-            pair = after(pair, *pieces[1:]) if True else pair
+            pair = after(pair, *pieces[1:])
             four = [*pair, *base_swap(pair, 1)]
             meant = sum(weights[k][:, None, None] * four[k] for k in range(4))
         *terms, residual = iterate(core_scalar, pieces, sky, other_sky, seen, place, column)
         last_one = iteration + 1 == ITERS
-        received = None if last_one else along_x(terms[1:])
+        if last_one:
+            terms, meant = lax.optimization_barrier((terms, meant))
+        received = along_x(terms[1:])
         if iteration:
-            sent = meant[1:3]
-            if 1 == 1:
-                sent = after(sent, terms[0])
-            elif 1 == 2 and not last_one:
-                sent = after(sent, *received)
-            came = band_swap(sent, 1)
+            came = band_swap(after(meant[1:3], terms[0]), 1)
             further = meant[3] + came[1]
-            if 0 == 1 and not last_one:
-                further = after(further, *received)
             consensus = meant[0] + came[0] + band_swap(further, 3)
             dual = dual + penalty * (jones - consensus)
             jones_next = jones - step_size * (dual + penalty * (jones - consensus))
         else:
             jones_next = jones
+        summed = terms[0] + received[0] + received[1] + received[2]
         if not last_one:
-            summed = terms[0] + received[0] + received[1] + received[2]
             others = along_z([summed] * 3)
             jones = jones_next + step_size * (summed + others[0] + others[1] + others[2])
     per_station = 2 * own_stations
-    leaving = jnp.stack([q.T.reshape(4, per_station, rows) for q in reorder(terms)], axis=1)
-    came = exchange(leaving.reshape(16 * per_station, rows)).reshape(16, per_station, rows)
+    here, there = residual[:, :base_dev], base_swap(residual[:, base_dev:], 1)
+    residual_out = jnp.where(core == 0, jnp.stack([here, there]), jnp.stack([there, here]))
+    turned_sum = summed.T
+    parts = [lax.dynamic_slice_in_dim(turned_sum, (z ^ k) * per_station, per_station, 0) for k in range(4)]
+    others = along_z(parts[1:])
+    residual_out, others = lax.optimization_barrier((residual_out, others))
     last = lax.dynamic_slice_in_dim(jones_next.T, z * per_station, per_station, 0)
-    last = last + step_size * jnp.sum(came, axis=0)
+    last = last + step_size * (parts[0] + others[0] + others[1] + others[2])
     last = last.reshape(2, own_stations, rows)
     kept, given = mine_of(last), base_swap(theirs_of(last), 1)
     both = jnp.where(core == 0, jnp.stack([kept, given]), jnp.stack([given, kept]))
     jones_out = both.reshape(sub_dev, own_stations, 8, dirs).transpose(0, 3, 2, 1)
-    here, there = residual[:, :base_dev], base_swap(residual[:, base_dev:], 1)
-    residual_out = jnp.where(core == 0, jnp.stack([here, there]), jnp.stack([there, here]))
     return (jones_out, residual_out)
 
 

time: 107 us -> 102 us (0.953)
  waiting for transfers between devices: 33.2 us -> 23.8 us
  starting transfers between devices: 60.1 us -> 66.4 us
  local copies, waits for them, and re-layouts: 5.1 us -> 3.49 us
    ppermute x26 -> x32, starting transfers between devices: 36.7 us -> 47.4 us  [base_swap(): lax.ppermute(value, 'base', [(i, i ^ mask) for i in range(base_count)])]
    all_to_all x2 -> x1, waiting for transfers between devices: 14.3 us -> 7.01 us  [exchange(): lax.all_to_all(value, 'base', 0, 0, axis_index_groups=plane_groups, tiled...]
    all_to_all x2 -> x1, starting transfers between devices: 12.7 us -> 6.45 us  [exchange(): lax.all_to_all(value, 'base', 0, 0, axis_index_groups=plane_groups, tiled...]
    ppermute x2, starting transfers between devices: 3.29 us -> 5.69 us  [per_device(): pair = jnp.stack([target, lax.ppermute(target, both_axes, across_z)])]
    ppermute x2, waiting for transfers between devices: 4.82 us -> 2.65 us  [per_device(): pair = jnp.stack([target, lax.ppermute(target, both_axes, across_z)])]
    ppermute x26 -> x32, waiting for transfers between devices: 13.1 us -> 12.9 us  [base_swap(): lax.ppermute(value, 'base', [(i, i ^ mask) for i in range(base_count)])]
  transfers between devices with their start and end apart: 34 -> 39, of which waited for: 15 -> 16; matrix products, arithmetic and copies ran while one was open for 6% -> 3% of each run, Pallas kernels for 2% -> 3%
where the time goes in v3:
time: 102 us
  starting transfers between devices  66.4 us (65%)
  waiting for transfers between devices  23.8 us (23%)
  Pallas kernels  4.01 us (4%)
  local copies, waits for them, and re-layouts  3.49 us (3%)
  other arithmetic  3.03 us (3%)
  between operations  1.03 us (1%)
    ppermute x32, starting transfers between devices, base_swap(): lax.ppermute(value, 'base', [(i, i ^ mask) for i in range(base_count)])  47.4 us
    ppermute x32, waiting for transfers between devices, base_swap(): lax.ppermute(value, 'base', [(i, i ^ mask) for i in range(base_count)])  12.9 us
    all_to_all x1, waiting for transfers between devices, exchange(): lax.all_to_all(value, 'base', 0, 0, axis_index_groups=plane_groups, tiled...  7.01 us
    ppermute x4, starting transfers between devices, band_swap(): lax.ppermute(value, 'band', [(i, i ^ mask) for i in range(band_count)])  6.86 us
    all_to_all x1, starting transfers between devices, exchange(): lax.all_to_all(value, 'base', 0, 0, axis_index_groups=plane_groups, tiled...  6.45 us
    ppermute x2, starting transfers between devices, per_device(): pair = jnp.stack([target, lax.ppermute(target, both_axes, across_z)])  5.69 us
    pallas_call x3, Pallas kernels, iterate(): pl.pallas_call(functools.partial(iteration_kernel, dirs), out_shape=[piec...  4.01 us
    ppermute x2, waiting for transfers between devices, per_device(): pair = jnp.stack([target, lax.ppermute(target, both_axes, across_z)])  2.65 us
  transfers between devices with their start and end apart: 39, of which 16 were waited for; matrix products, arithmetic and copies ran while one was open for 3% of the time, Pallas kernels for 3%

profile of v3, /device:TPU:1, one launch (start us, length us, event | category | flops | bytes accessed | tf_op | source)
XLA Modules:
  0.0 101.7 jit_solution(12871636399514997757)
XLA Ops:
  1.7 3.3 %collective-permute-start = (f32[16,128]{1,0:T(8,128)S(1)}, f32[16,128]{1,0:T(8,128)S(1)}, u32[]{:S(2)}, u32[]{:S(2)}) collective-permute-start(f32[16,128]{1,0:T(8,128)S(1)} %select_n.204), channel_id=1, source_target_pairs={{0,8},{8,0},{16,24},{24,16},{32,40},{40,32},{48,56},{56,48},{64,72... | collective-permute-start | bytes 24584 | tf_op jit(solution)/shard_map/ppermute | solution.py:176
  6.7 6.4 %all-to-all-start = ((f32[16,32,128]{2,1,0:T(8,128)}), f32[16,32,128]{2,1,0:T(8,128)S(1)}, u32[]{:S(2)}, u32[]{:S(2)}) async-start(f32[16,32,128]{2,1,0:T(8,128)} %broadcast_in_dim.10), calls=%async_computation | async-start | bytes 524288 | tf_op jit(solution)/shard_map/all_to_all | solution.py:196
  16.1 7.0 %all-to-all-done = f32[16,32,128]{2,1,0:T(8,128)S(1)} async-done(((f32[16,32,128]{2,1,0:T(8,128)}), f32[16,32,128]{2,1,0:T(8,128)S(1)}, u32[]{:S(2)}, u32[]{:S(2)}) %all-to-all-start) | async-done | bytes 262176 | tf_op jit(solution)/shard_map/all_to_all | solution.py:196
  23.6 1.4 %shard_map.77 = (f32[128,128]{1,0:T(8,128)S(1)}, f32[128,128]{1,0:T(8,128)S(1)}, f32[128,128]{1,0:T(8,128)S(1)}, f32[128,128]{1,0:T(8,128)S(1)}, f32[8,512]{1,0:T(8,128)}) custom-call(s32[1]{0:T(128)} %bitcast.8.core_ref, f32[128,128]{1,0:T(8,128)S(1)} %get-tuple-element.37.j0, f32[128,128]{1,0:T(8,128)S(1)} %get-tuple-element.99.j1, ...), custom_call_target="tpu_custom_call" | custom-call | flops 536870912 | bytes 2097152 | tf_op jit(solution)/shard_map/pallas_call | solution.py:143
  25.1 2.1 %collective-permute-start.5 = (f32[128,128]{1,0:T(8,128)S(1)}, f32[128,128]{1,0:T(8,128)S(1)}, u32[]{:S(2)}, u32[]{:S(2)}) collective-permute-start(f32[128,128]{1,0:T(8,128)S(1)} %get-tuple-element.44), channel_id=1, source_target_pairs={{0,32},{8,40},{16,48},{24,56},{32,0},{40,8},{48,16},{56,24},{64,96... | collective-permute-start | bytes 196616 | tf_op jit(solution)/shard_map/ppermute | solution.py:176
  30.7 1.7 %collective-permute-start.9 = (f32[128,128]{1,0:T(8,128)S(1)}, f32[128,128]{1,0:T(8,128)S(1)}, u32[]{:S(2)}, u32[]{:S(2)}) collective-permute-start(f32[128,128]{1,0:T(8,128)S(1)} %add_add_fusion.3), channel_id=1, source_target_pairs={{0,192},{8,200},{16,208},{24,216},{32,224},{40,232},{48,240},{56,2... | collective-permute-start | bytes 196616 | tf_op jit(solution)/shard_map/ppermute | solution.py:176
  32.6 1.8 %collective-permute-start.7 = (f32[128,128]{1,0:T(8,128)S(1)}, f32[128,128]{1,0:T(8,128)S(1)}, u32[]{:S(2)}, u32[]{:S(2)}) collective-permute-start(f32[128,128]{1,0:T(8,128)S(1)} %add_add_fusion.3), channel_id=1, source_target_pairs={{0,64},{8,72},{16,80},{24,88},{32,96},{40,104},{48,112},{56,120},{... | collective-permute-start | bytes 196616 | tf_op jit(solution)/shard_map/ppermute | solution.py:176
  35.7 1.7 %collective-permute-done.8 = f32[128,128]{1,0:T(8,128)S(1)} collective-permute-done((f32[128,128]{1,0:T(8,128)S(1)}, f32[128,128]{1,0:T(8,128)S(1)}, u32[]{:S(2)}, u32[]{:S(2)}) %collective-permute-start.8) | collective-permute-done | bytes 65568 | tf_op jit(solution)/shard_map/ppermute | solution.py:176
  38.0 2.6 %collective-permute-start.12 = (f32[128,128]{1,0:T(8,128)S(1)}, f32[128,128]{1,0:T(8,128)S(1)}, u32[]{:S(2)}, u32[]{:S(2)}) collective-permute-start(f32[128,128]{1,0:T(8,128)S(1)} %multiply_add_fusion.3.j0), channel_id=1, source_target_pairs={{0,32},{8,40},{16,48},{24,56},{32,0},{40,8},{48,16},{56,24},{64,96... | collective-permute-start | bytes 196616 | tf_op jit(solution)/shard_map/ppermute | solution.py:176
  41.4 2.8 %collective-permute-start.10 = (f32[128,128]{1,0:T(8,128)S(1)}, f32[128,128]{1,0:T(8,128)S(1)}, u32[]{:S(2)}, u32[]{:S(2)}) collective-permute-start(f32[128,128]{1,0:T(8,128)S(1)} %multiply_add_fusion.3.j0), channel_id=1, source_target_pairs={{0,196},{1,197},{2,198},{3,199},{4,192},{5,193},{6,194},{7,195},{8... | collective-permute-start | bytes 196616 | tf_op jit(solution)/shard_map/ppermute | solution.py:242
  47.2 2.5 %collective-permute-start.17 = (f32[128,128]{1,0:T(8,128)S(1)}, f32[128,128]{1,0:T(8,128)S(1)}, u32[]{:S(2)}, u32[]{:S(2)}) collective-permute-start(f32[128,128]{1,0:T(8,128)S(1)} %get-tuple-element.53), channel_id=1, source_target_pairs={{0,16},{8,24},{16,0},{24,8},{32,48},{40,56},{48,32},{56,40},{64,80... | collective-permute-start | bytes 196616 | tf_op jit(solution)/shard_map/ppermute | solution.py:176
  49.6 6.4 %collective-permute-start.14 = (f32[2,128,128]{2,1,0:T(8,128)S(1)}, f32[2,128,128]{2,1,0:T(8,128)S(1)}, u32[]{:S(2)}, u32[]{:S(2)}) collective-permute-start(f32[2,128,128]{2,1,0:T(8,128)S(1)} %pad_maximum_fusion), channel_id=1, source_target_pairs={{0,8},{8,0},{16,24},{24,16},{32,40},{40,32},{48,56},{56,48},{64,72... | collective-permute-start | bytes 393224 | tf_op jit(solution)/shard_map/ppermute | solution.py:176
  62.3 2.6 %collective-permute-start.16 = (f32[128,128]{1,0:T(8,128)S(1)}, f32[128,128]{1,0:T(8,128)S(1)}, u32[]{:S(2)}, u32[]{:S(2)}) collective-permute-start(f32[128,128]{1,0:T(8,128)S(1)} %fusion.9), channel_id=1, source_target_pairs={{0,3},{1,2},{2,1},{3,0},{4,7},{5,6},{6,5},{7,4},{8,11},{9,10},{10,... | collective-permute-start | bytes 196616 | tf_op jit(solution)/shard_map/ppermute | solution.py:179
  64.8 2.6 %collective-permute-done.21 = f32[128,128]{1,0:T(8,128)S(1)} collective-permute-done((f32[128,128]{1,0:T(8,128)S(1)}, f32[128,128]{1,0:T(8,128)S(1)}, u32[]{:S(2)}, u32[]{:S(2)}) %collective-permute-start.21) | collective-permute-done | bytes 65568 | tf_op jit(solution)/shard_map/ppermute | solution.py:176
  67.6 1.8 %collective-permute-start.24 = (f32[128,128]{1,0:T(8,128)S(1)}, f32[128,128]{1,0:T(8,128)S(1)}, u32[]{:S(2)}, u32[]{:S(2)}) collective-permute-start(f32[128,128]{1,0:T(8,128)S(1)} %get-tuple-element.73.j0), channel_id=1, source_target_pairs={{0,32},{8,40},{16,48},{24,56},{32,0},{40,8},{48,16},{56,24},{64,96... | collective-permute-start | bytes 196616 | tf_op jit(solution)/shard_map/ppermute | solution.py:176
  69.4 2.0 %collective-permute-start.25 = (f32[128,128]{1,0:T(8,128)S(1)}, f32[128,128]{1,0:T(8,128)S(1)}, u32[]{:S(2)}, u32[]{:S(2)}) collective-permute-start(f32[128,128]{1,0:T(8,128)S(1)} %get-tuple-element.73.j0), channel_id=1, source_target_pairs={{0,48},{8,56},{16,32},{24,40},{32,16},{40,24},{48,0},{56,8},{64,11... | collective-permute-start | bytes 196616 | tf_op jit(solution)/shard_map/ppermute | solution.py:176
  71.4 2.9 %collective-permute-start.26 = (f32[128,128]{1,0:T(8,128)S(1)}, f32[128,128]{1,0:T(8,128)S(1)}, u32[]{:S(2)}, u32[]{:S(2)}) collective-permute-start(f32[128,128]{1,0:T(8,128)S(1)} %get-tuple-element.72), channel_id=1, source_target_pairs={{0,196},{1,197},{2,198},{3,199},{4,192},{5,193},{6,194},{7,195},{8... | collective-permute-start | bytes 196616 | tf_op jit(solution)/shard_map/ppermute | solution.py:242
  74.3 2.6 %collective-permute-done.26 = f32[128,128]{1,0:T(8,128)S(1)} collective-permute-done((f32[128,128]{1,0:T(8,128)S(1)}, f32[128,128]{1,0:T(8,128)S(1)}, u32[]{:S(2)}, u32[]{:S(2)}) %collective-permute-start.26) | collective-permute-done | bytes 65568 | tf_op jit(solution)/shard_map/ppermute | solution.py:242
  77.0 2.7 %collective-permute-start.27 = (f32[2,128,128]{2,1,0:T(8,128)S(1)}, f32[2,128,128]{2,1,0:T(8,128)S(1)}, u32[]{:S(2)}, u32[]{:S(2)}) collective-permute-start(f32[2,128,128]{2,1,0:T(8,128)S(1)} %pad_maximum_fusion.1), channel_id=1, source_target_pairs={{0,8},{8,0},{16,24},{24,16},{32,40},{40,32},{48,56},{56,48},{64,72... | collective-permute-start | bytes 393224 | tf_op jit(solution)/shard_map/ppermute | solution.py:176
  82.5 1.9 %collective-permute-start.30 = (f32[128,128]{1,0:T(8,128)S(1)}, f32[128,128]{1,0:T(8,128)S(1)}, u32[]{:S(2)}, u32[]{:S(2)}) collective-permute-start(f32[128,128]{1,0:T(8,128)S(1)} %get-tuple-element.64), channel_id=1, source_target_pairs={{0,16},{8,24},{16,0},{24,8},{32,48},{40,56},{48,32},{56,40},{64,80... | collective-permute-start | bytes 196616 | tf_op jit(solution)/shard_map/ppermute | solution.py:176
  87.5 2.7 %collective-permute-start.34 = (f32[32,128]{0,1:T(8,128)S(1)}, f32[32,128]{0,1:T(8,128)S(1)}, u32[]{:S(2)}, u32[]{:S(2)}) collective-permute-start(f32[32,128]{0,1:T(8,128)S(1)} %get-tuple-element.93), channel_id=1, source_target_pairs={{0,64},{8,72},{16,80},{24,88},{32,96},{40,104},{48,112},{56,120},{... | collective-permute-start | bytes 49160 | tf_op jit(solution)/shard_map/ppermute | solution.py:176
  90.3 2.0 %collective-permute-start.36 = (f32[32,128]{0,1:T(8,128)S(1)}, f32[32,128]{0,1:T(8,128)S(1)}, u32[]{:S(2)}, u32[]{:S(2)}) collective-permute-start(f32[32,128]{0,1:T(8,128)S(1)} %get-tuple-element.91), channel_id=1, source_target_pairs={{0,192},{8,200},{16,208},{24,216},{32,224},{40,232},{48,240},{56,2... | collective-permute-start | bytes 49160 | tf_op jit(solution)/shard_map/ppermute | solution.py:176
  92.3 2.8 %collective-permute-start.29 = (f32[128,128]{1,0:T(8,128)S(1)}, f32[128,128]{1,0:T(8,128)S(1)}, u32[]{:S(2)}, u32[]{:S(2)}) collective-permute-start(f32[128,128]{1,0:T(8,128)S(1)} %fusion.6), channel_id=1, source_target_pairs={{0,3},{1,2},{2,1},{3,0},{4,7},{5,6},{6,5},{7,4},{8,11},{9,10},{10,... | collective-permute-start | bytes 196616 | tf_op jit(solution)/shard_map/ppermute | solution.py:179
  97.2 2.9 %collective-permute-start.37 = (f32[16,128]{0,1:T(8,128)S(1)}, f32[16,128]{0,1:T(8,128)S(1)}, u32[]{:S(2)}, u32[]{:S(2)}) collective-permute-start(f32[16,128]{0,1:T(8,128)S(1)} %get-tuple-element.90), channel_id=1, source_target_pairs={{0,8},{8,0},{16,24},{24,16},{32,40},{40,32},{48,56},{56,48},{64,72... | collective-permute-start | bytes 24584 | tf_op jit(solution)/shard_map/ppermute | solution.py:176
  (118 shorter events, 31.4 us)
Async XLA Ops:
  6.7 16.4 %all-to-all-start = ((f32[16,32,128]{2,1,0:T(8,128)}), f32[16,32,128]{2,1,0:T(8,128)S(1)}, u32[]{:S(2)}, u32[]{:S(2)}) async-start(f32[16,32,128]{2,1,0:T(8,128)} %broadcast_in_dim.10), calls=%async_computation | async-start | bytes 524288 | tf_op jit(solution)/shard_map/all_to_all | solution.py:196
  13.2 10.4 %collective-permute-start.1 = (f32[128,256]{1,0:T(8,128)S(1)}, f32[128,256]{1,0:T(8,128)S(1)}, u32[]{:S(2)}, u32[]{:S(2)}) collective-permute-start(f32[128,256]{1,0:T(8,128)S(1)} %bitcast.120), channel_id=1, source_target_pairs={{0,8},{8,0},{16,24},{24,16},{32,40},{40,32},{48,56},{56,48},{64,72... | collective-permute-start | bytes 393224 | tf_op jit(solution)/shard_map/ppermute | solution.py:176
  30.7 5.0 %collective-permute-start.9 = (f32[128,128]{1,0:T(8,128)S(1)}, f32[128,128]{1,0:T(8,128)S(1)}, u32[]{:S(2)}, u32[]{:S(2)}) collective-permute-start(f32[128,128]{1,0:T(8,128)S(1)} %add_add_fusion.3), channel_id=1, source_target_pairs={{0,192},{8,200},{16,208},{24,216},{32,224},{40,232},{48,240},{56,2... | collective-permute-start | bytes 196616 | tf_op jit(solution)/shard_map/ppermute | solution.py:176
  37.5 6.7 %collective-permute-start.11 = (f32[128,128]{1,0:T(8,128)S(1)}, f32[128,128]{1,0:T(8,128)S(1)}, u32[]{:S(2)}, u32[]{:S(2)}) collective-permute-start(f32[128,128]{1,0:T(8,128)S(1)} %multiply_add_fusion.3.j0), channel_id=1, source_target_pairs={{0,16},{8,24},{16,0},{24,8},{32,48},{40,56},{48,32},{56,40},{64,80... | collective-permute-start | bytes 196616 | tf_op jit(solution)/shard_map/ppermute | solution.py:176
  38.0 6.2 %collective-permute-start.12 = (f32[128,128]{1,0:T(8,128)S(1)}, f32[128,128]{1,0:T(8,128)S(1)}, u32[]{:S(2)}, u32[]{:S(2)}) collective-permute-start(f32[128,128]{1,0:T(8,128)S(1)} %multiply_add_fusion.3.j0), channel_id=1, source_target_pairs={{0,32},{8,40},{16,48},{24,56},{32,0},{40,8},{48,16},{56,24},{64,96... | collective-permute-start | bytes 196616 | tf_op jit(solution)/shard_map/ppermute | solution.py:176
  41.4 8.2 %collective-permute-start.10 = (f32[128,128]{1,0:T(8,128)S(1)}, f32[128,128]{1,0:T(8,128)S(1)}, u32[]{:S(2)}, u32[]{:S(2)}) collective-permute-start(f32[128,128]{1,0:T(8,128)S(1)} %multiply_add_fusion.3.j0), channel_id=1, source_target_pairs={{0,196},{1,197},{2,198},{3,199},{4,192},{5,193},{6,194},{7,195},{8... | collective-permute-start | bytes 196616 | tf_op jit(solution)/shard_map/ppermute | solution.py:242
  46.4 12.2 %collective-permute-start.19 = (f32[128,128]{1,0:T(8,128)S(1)}, f32[128,128]{1,0:T(8,128)S(1)}, u32[]{:S(2)}, u32[]{:S(2)}) collective-permute-start(f32[128,128]{1,0:T(8,128)S(1)} %get-tuple-element.55), channel_id=1, source_target_pairs={{0,48},{8,56},{16,32},{24,40},{32,16},{40,24},{48,0},{56,8},{64,11... | collective-permute-start | bytes 196616 | tf_op jit(solution)/shard_map/ppermute | solution.py:176
  47.1 11.4 %collective-permute-start.18 = (f32[128,128]{1,0:T(8,128)S(1)}, f32[128,128]{1,0:T(8,128)S(1)}, u32[]{:S(2)}, u32[]{:S(2)}) collective-permute-start(f32[128,128]{1,0:T(8,128)S(1)} %get-tuple-element.54), channel_id=1, source_target_pairs={{0,32},{8,40},{16,48},{24,56},{32,0},{40,8},{48,16},{56,24},{64,96... | collective-permute-start | bytes 196616 | tf_op jit(solution)/shard_map/ppermute | solution.py:176
  47.2 11.4 %collective-permute-start.17 = (f32[128,128]{1,0:T(8,128)S(1)}, f32[128,128]{1,0:T(8,128)S(1)}, u32[]{:S(2)}, u32[]{:S(2)}) collective-permute-start(f32[128,128]{1,0:T(8,128)S(1)} %get-tuple-element.53), channel_id=1, source_target_pairs={{0,16},{8,24},{16,0},{24,8},{32,48},{40,56},{48,32},{56,40},{64,80... | collective-permute-start | bytes 196616 | tf_op jit(solution)/shard_map/ppermute | solution.py:176
  49.6 7.4 %collective-permute-start.14 = (f32[2,128,128]{2,1,0:T(8,128)S(1)}, f32[2,128,128]{2,1,0:T(8,128)S(1)}, u32[]{:S(2)}, u32[]{:S(2)}) collective-permute-start(f32[2,128,128]{2,1,0:T(8,128)S(1)} %pad_maximum_fusion), channel_id=1, source_target_pairs={{0,8},{8,0},{16,24},{24,16},{32,40},{40,32},{48,56},{56,48},{64,72... | collective-permute-start | bytes 393224 | tf_op jit(solution)/shard_map/ppermute | solution.py:176
  57.2 5.1 %collective-permute-start.15 = (f32[2,128,128]{2,1,0:T(8,128)S(1)}, f32[2,128,128]{2,1,0:T(8,128)S(1)}, u32[]{:S(2)}, u32[]{:S(2)}) collective-permute-start(f32[2,128,128]{2,1,0:T(8,128)S(1)} %slice.137), channel_id=1, source_target_pairs={{0,1},{1,0},{2,3},{3,2},{4,5},{5,4},{6,7},{7,6},{8,9},{9,8},{10,11... | collective-permute-start | bytes 393224 | tf_op jit(solution)/shard_map/ppermute | solution.py:179
  58.6 6.2 %collective-permute-start.22 = (f32[128,128]{1,0:T(8,128)S(1)}, f32[128,128]{1,0:T(8,128)S(1)}, u32[]{:S(2)}, u32[]{:S(2)}) collective-permute-start(f32[128,128]{1,0:T(8,128)S(1)} %add_add_fusion.2), channel_id=1, source_target_pairs={{0,192},{8,200},{16,208},{24,216},{32,224},{40,232},{48,240},{56,2... | collective-permute-start | bytes 196616 | tf_op jit(solution)/shard_map/ppermute | solution.py:176
  59.9 7.5 %collective-permute-start.21 = (f32[128,128]{1,0:T(8,128)S(1)}, f32[128,128]{1,0:T(8,128)S(1)}, u32[]{:S(2)}, u32[]{:S(2)}) collective-permute-start(f32[128,128]{1,0:T(8,128)S(1)} %add_add_fusion.2), channel_id=1, source_target_pairs={{0,128},{8,136},{16,144},{24,152},{32,160},{40,168},{48,176},{56,1... | collective-permute-start | bytes 196616 | tf_op jit(solution)/shard_map/ppermute | solution.py:176
  60.9 6.5 %collective-permute-start.20 = (f32[128,128]{1,0:T(8,128)S(1)}, f32[128,128]{1,0:T(8,128)S(1)}, u32[]{:S(2)}, u32[]{:S(2)}) collective-permute-start(f32[128,128]{1,0:T(8,128)S(1)} %add_add_fusion.2), channel_id=1, source_target_pairs={{0,64},{8,72},{16,80},{24,88},{32,96},{40,104},{48,112},{56,120},{... | collective-permute-start | bytes 196616 | tf_op jit(solution)/shard_map/ppermute | solution.py:176
  62.3 5.2 %collective-permute-start.16 = (f32[128,128]{1,0:T(8,128)S(1)}, f32[128,128]{1,0:T(8,128)S(1)}, u32[]{:S(2)}, u32[]{:S(2)}) collective-permute-start(f32[128,128]{1,0:T(8,128)S(1)} %fusion.9), channel_id=1, source_target_pairs={{0,3},{1,2},{2,1},{3,0},{4,7},{5,6},{6,5},{7,4},{8,11},{9,10},{10,... | collective-permute-start | bytes 196616 | tf_op jit(solution)/shard_map/ppermute | solution.py:179
  67.5 9.5 %collective-permute-start.23 = (f32[128,128]{1,0:T(8,128)S(1)}, f32[128,128]{1,0:T(8,128)S(1)}, u32[]{:S(2)}, u32[]{:S(2)}) collective-permute-start(f32[128,128]{1,0:T(8,128)S(1)} %get-tuple-element.73.j0), channel_id=1, source_target_pairs={{0,16},{8,24},{16,0},{24,8},{32,48},{40,56},{48,32},{56,40},{64,80... | collective-permute-start | bytes 196616 | tf_op jit(solution)/shard_map/ppermute | solution.py:176
  67.6 9.4 %collective-permute-start.24 = (f32[128,128]{1,0:T(8,128)S(1)}, f32[128,128]{1,0:T(8,128)S(1)}, u32[]{:S(2)}, u32[]{:S(2)}) collective-permute-start(f32[128,128]{1,0:T(8,128)S(1)} %get-tuple-element.73.j0), channel_id=1, source_target_pairs={{0,32},{8,40},{16,48},{24,56},{32,0},{40,8},{48,16},{56,24},{64,96... | collective-permute-start | bytes 196616 | tf_op jit(solution)/shard_map/ppermute | solution.py:176
  69.4 7.6 %collective-permute-start.25 = (f32[128,128]{1,0:T(8,128)S(1)}, f32[128,128]{1,0:T(8,128)S(1)}, u32[]{:S(2)}, u32[]{:S(2)}) collective-permute-start(f32[128,128]{1,0:T(8,128)S(1)} %get-tuple-element.73.j0), channel_id=1, source_target_pairs={{0,48},{8,56},{16,32},{24,40},{32,16},{40,24},{48,0},{56,8},{64,11... | collective-permute-start | bytes 196616 | tf_op jit(solution)/shard_map/ppermute | solution.py:176
  71.4 5.5 %collective-permute-start.26 = (f32[128,128]{1,0:T(8,128)S(1)}, f32[128,128]{1,0:T(8,128)S(1)}, u32[]{:S(2)}, u32[]{:S(2)}) collective-permute-start(f32[128,128]{1,0:T(8,128)S(1)} %get-tuple-element.72), channel_id=1, source_target_pairs={{0,196},{1,197},{2,198},{3,199},{4,192},{5,193},{6,194},{7,195},{8... | collective-permute-start | bytes 196616 | tf_op jit(solution)/shard_map/ppermute | solution.py:242
  84.4 10.7 %collective-permute-start.33 = (f32[8,256]{1,0:T(8,128)S(1)}, f32[8,256]{1,0:T(8,128)S(1)}, u32[]{:S(2)}, u32[]{:S(2)}) collective-permute-start(f32[8,256]{1,0:T(8,128)S(1)} %get-tuple-element.95), channel_id=1, source_target_pairs={{0,8},{8,0},{16,24},{24,16},{32,40},{40,32},{48,56},{56,48},{64,72... | collective-permute-start | bytes 24584 | tf_op jit(solution)/shard_map/ppermute | solution.py:176
  85.5 6.9 %collective-permute-start.28 = (f32[2,128,128]{2,1,0:T(8,128)S(1)}, f32[2,128,128]{2,1,0:T(8,128)S(1)}, u32[]{:S(2)}, u32[]{:S(2)}) collective-permute-start(f32[2,128,128]{2,1,0:T(8,128)S(1)} %slice.120), channel_id=1, source_target_pairs={{0,1},{1,0},{2,3},{3,2},{4,5},{5,4},{6,7},{7,6},{8,9},{9,8},{10,11... | collective-permute-start | bytes 393224 | tf_op jit(solution)/shard_map/ppermute | solution.py:179
  87.5 8.3 %collective-permute-start.34 = (f32[32,128]{0,1:T(8,128)S(1)}, f32[32,128]{0,1:T(8,128)S(1)}, u32[]{:S(2)}, u32[]{:S(2)}) collective-permute-start(f32[32,128]{0,1:T(8,128)S(1)} %get-tuple-element.93), channel_id=1, source_target_pairs={{0,64},{8,72},{16,80},{24,88},{32,96},{40,104},{48,112},{56,120},{... | collective-permute-start | bytes 49160 | tf_op jit(solution)/shard_map/ppermute | solution.py:176
  90.1 5.6 %collective-permute-start.35 = (f32[32,128]{0,1:T(8,128)S(1)}, f32[32,128]{0,1:T(8,128)S(1)}, u32[]{:S(2)}, u32[]{:S(2)}) collective-permute-start(f32[32,128]{0,1:T(8,128)S(1)} %get-tuple-element.92), channel_id=1, source_target_pairs={{0,128},{8,136},{16,144},{24,152},{32,160},{40,168},{48,176},{56,1... | collective-permute-start | bytes 49160 | tf_op jit(solution)/shard_map/ppermute | solution.py:176
  90.3 5.5 %collective-permute-start.36 = (f32[32,128]{0,1:T(8,128)S(1)}, f32[32,128]{0,1:T(8,128)S(1)}, u32[]{:S(2)}, u32[]{:S(2)}) collective-permute-start(f32[32,128]{0,1:T(8,128)S(1)} %get-tuple-element.91), channel_id=1, source_target_pairs={{0,192},{8,200},{16,208},{24,216},{32,224},{40,232},{48,240},{56,2... | collective-permute-start | bytes 49160 | tf_op jit(solution)/shard_map/ppermute | solution.py:176
  (19 other events, 68.3 us)

commit v4 on v3

--- a/solution.py
+++ b/solution.py
@@ -246,7 +246,7 @@
         *terms, residual = iterate(core_scalar, pieces, sky, other_sky, seen, place, column)
         last_one = iteration + 1 == ITERS
         if last_one:
-            terms, meant = lax.optimization_barrier((terms, meant))
+            terms, residual, meant = lax.optimization_barrier((terms, residual, meant))
         received = along_x(terms[1:])
         if iteration:
             came = band_swap(after(meant[1:3], terms[0]), 1)

time: 102 us -> 102 us (level)
  no operation moved by 1% of the time
where the time goes in v4:
time: 102 us
  starting transfers between devices  66.4 us (65%)
  waiting for transfers between devices  23.9 us (23%)
  Pallas kernels  4.01 us (4%)
  local copies, waits for them, and re-layouts  3.49 us (3%)
  other arithmetic  3.03 us (3%)
  between operations  1.03 us (1%)
    ppermute x32, starting transfers between devices, base_swap(): lax.ppermute(value, 'base', [(i, i ^ mask) for i in range(base_count)])  47.1 us
    ppermute x32, waiting for transfers between devices, base_swap(): lax.ppermute(value, 'base', [(i, i ^ mask) for i in range(base_count)])  13.1 us
    ppermute x4, starting transfers between devices, band_swap(): lax.ppermute(value, 'band', [(i, i ^ mask) for i in range(band_count)])  7.17 us
    all_to_all x1, waiting for transfers between devices, exchange(): lax.all_to_all(value, 'base', 0, 0, axis_index_groups=plane_groups, tiled...  7.01 us
    all_to_all x1, starting transfers between devices, exchange(): lax.all_to_all(value, 'base', 0, 0, axis_index_groups=plane_groups, tiled...  6.45 us
    ppermute x2, starting transfers between devices, per_device(): pair = jnp.stack([target, lax.ppermute(target, both_axes, across_z)])  5.69 us
    pallas_call x3, Pallas kernels, iterate(): pl.pallas_call(functools.partial(iteration_kernel, dirs), out_shape=[piec...  4.01 us
    ppermute x2, waiting for transfers between devices, per_device(): pair = jnp.stack([target, lax.ppermute(target, both_axes, across_z)])  2.65 us
  transfers between devices with their start and end apart: 39, of which 16 were waited for; matrix products, arithmetic and copies ran while one was open for 3% of the time, Pallas kernels for 3%

profile of v4, /device:TPU:1, one launch (start us, length us, event | category | flops | bytes accessed | tf_op | source)
XLA Modules:
  0.0 101.8 jit_solution(12921306953097082018)
XLA Ops:
  1.7 3.3 %collective-permute-start = (f32[16,128]{1,0:T(8,128)S(1)}, f32[16,128]{1,0:T(8,128)S(1)}, u32[]{:S(2)}, u32[]{:S(2)}) collective-permute-start(f32[16,128]{1,0:T(8,128)S(1)} %select_n.204), channel_id=1, source_target_pairs={{0,8},{8,0},{16,24},{24,16},{32,40},{40,32},{48,56},{56,48},{64,72... | collective-permute-start | bytes 24584 | tf_op jit(solution)/shard_map/ppermute | solution.py:176
  6.7 6.4 %all-to-all-start = ((f32[16,32,128]{2,1,0:T(8,128)}), f32[16,32,128]{2,1,0:T(8,128)S(1)}, u32[]{:S(2)}, u32[]{:S(2)}) async-start(f32[16,32,128]{2,1,0:T(8,128)} %broadcast_in_dim.10), calls=%async_computation | async-start | bytes 524288 | tf_op jit(solution)/shard_map/all_to_all | solution.py:196
  16.1 7.0 %all-to-all-done = f32[16,32,128]{2,1,0:T(8,128)S(1)} async-done(((f32[16,32,128]{2,1,0:T(8,128)}), f32[16,32,128]{2,1,0:T(8,128)S(1)}, u32[]{:S(2)}, u32[]{:S(2)}) %all-to-all-start) | async-done | bytes 262176 | tf_op jit(solution)/shard_map/all_to_all | solution.py:196
  23.6 1.4 %shard_map.77 = (f32[128,128]{1,0:T(8,128)S(1)}, f32[128,128]{1,0:T(8,128)S(1)}, f32[128,128]{1,0:T(8,128)S(1)}, f32[128,128]{1,0:T(8,128)S(1)}, f32[8,512]{1,0:T(8,128)}) custom-call(s32[1]{0:T(128)} %bitcast.8.core_ref, f32[128,128]{1,0:T(8,128)S(1)} %get-tuple-element.38.j0, f32[128,128]{1,0:T(8,128)S(1)} %get-tuple-element.101.j1, ...), custom_call_target="tpu_custom_call" | custom-call | flops 536870912 | bytes 2097152 | tf_op jit(solution)/shard_map/pallas_call | solution.py:143
  25.1 2.1 %collective-permute-start.5 = (f32[128,128]{1,0:T(8,128)S(1)}, f32[128,128]{1,0:T(8,128)S(1)}, u32[]{:S(2)}, u32[]{:S(2)}) collective-permute-start(f32[128,128]{1,0:T(8,128)S(1)} %get-tuple-element.45), channel_id=1, source_target_pairs={{0,32},{8,40},{16,48},{24,56},{32,0},{40,8},{48,16},{56,24},{64,96... | collective-permute-start | bytes 196616 | tf_op jit(solution)/shard_map/ppermute | solution.py:176
  30.7 1.7 %collective-permute-start.9 = (f32[128,128]{1,0:T(8,128)S(1)}, f32[128,128]{1,0:T(8,128)S(1)}, u32[]{:S(2)}, u32[]{:S(2)}) collective-permute-start(f32[128,128]{1,0:T(8,128)S(1)} %add_add_fusion.3), channel_id=1, source_target_pairs={{0,192},{8,200},{16,208},{24,216},{32,224},{40,232},{48,240},{56,2... | collective-permute-start | bytes 196616 | tf_op jit(solution)/shard_map/ppermute | solution.py:176
  32.6 1.8 %collective-permute-start.7 = (f32[128,128]{1,0:T(8,128)S(1)}, f32[128,128]{1,0:T(8,128)S(1)}, u32[]{:S(2)}, u32[]{:S(2)}) collective-permute-start(f32[128,128]{1,0:T(8,128)S(1)} %add_add_fusion.3), channel_id=1, source_target_pairs={{0,64},{8,72},{16,80},{24,88},{32,96},{40,104},{48,112},{56,120},{... | collective-permute-start | bytes 196616 | tf_op jit(solution)/shard_map/ppermute | solution.py:176
  35.7 1.7 %collective-permute-done.8 = f32[128,128]{1,0:T(8,128)S(1)} collective-permute-done((f32[128,128]{1,0:T(8,128)S(1)}, f32[128,128]{1,0:T(8,128)S(1)}, u32[]{:S(2)}, u32[]{:S(2)}) %collective-permute-start.8) | collective-permute-done | bytes 65568 | tf_op jit(solution)/shard_map/ppermute | solution.py:176
  38.0 2.6 %collective-permute-start.12 = (f32[128,128]{1,0:T(8,128)S(1)}, f32[128,128]{1,0:T(8,128)S(1)}, u32[]{:S(2)}, u32[]{:S(2)}) collective-permute-start(f32[128,128]{1,0:T(8,128)S(1)} %multiply_add_fusion.3.j0), channel_id=1, source_target_pairs={{0,32},{8,40},{16,48},{24,56},{32,0},{40,8},{48,16},{56,24},{64,96... | collective-permute-start | bytes 196616 | tf_op jit(solution)/shard_map/ppermute | solution.py:176
  41.4 2.8 %collective-permute-start.10 = (f32[128,128]{1,0:T(8,128)S(1)}, f32[128,128]{1,0:T(8,128)S(1)}, u32[]{:S(2)}, u32[]{:S(2)}) collective-permute-start(f32[128,128]{1,0:T(8,128)S(1)} %multiply_add_fusion.3.j0), channel_id=1, source_target_pairs={{0,196},{1,197},{2,198},{3,199},{4,192},{5,193},{6,194},{7,195},{8... | collective-permute-start | bytes 196616 | tf_op jit(solution)/shard_map/ppermute | solution.py:242
  47.2 2.5 %collective-permute-start.17 = (f32[128,128]{1,0:T(8,128)S(1)}, f32[128,128]{1,0:T(8,128)S(1)}, u32[]{:S(2)}, u32[]{:S(2)}) collective-permute-start(f32[128,128]{1,0:T(8,128)S(1)} %get-tuple-element.54), channel_id=1, source_target_pairs={{0,16},{8,24},{16,0},{24,8},{32,48},{40,56},{48,32},{56,40},{64,80... | collective-permute-start | bytes 196616 | tf_op jit(solution)/shard_map/ppermute | solution.py:176
  49.6 6.4 %collective-permute-start.14 = (f32[2,128,128]{2,1,0:T(8,128)S(1)}, f32[2,128,128]{2,1,0:T(8,128)S(1)}, u32[]{:S(2)}, u32[]{:S(2)}) collective-permute-start(f32[2,128,128]{2,1,0:T(8,128)S(1)} %pad_maximum_fusion), channel_id=1, source_target_pairs={{0,8},{8,0},{16,24},{24,16},{32,40},{40,32},{48,56},{56,48},{64,72... | collective-permute-start | bytes 393224 | tf_op jit(solution)/shard_map/ppermute | solution.py:176
  62.3 2.6 %collective-permute-start.16 = (f32[128,128]{1,0:T(8,128)S(1)}, f32[128,128]{1,0:T(8,128)S(1)}, u32[]{:S(2)}, u32[]{:S(2)}) collective-permute-start(f32[128,128]{1,0:T(8,128)S(1)} %fusion.9), channel_id=1, source_target_pairs={{0,3},{1,2},{2,1},{3,0},{4,7},{5,6},{6,5},{7,4},{8,11},{9,10},{10,... | collective-permute-start | bytes 196616 | tf_op jit(solution)/shard_map/ppermute | solution.py:179
  64.8 2.6 %collective-permute-done.21 = f32[128,128]{1,0:T(8,128)S(1)} collective-permute-done((f32[128,128]{1,0:T(8,128)S(1)}, f32[128,128]{1,0:T(8,128)S(1)}, u32[]{:S(2)}, u32[]{:S(2)}) %collective-permute-start.21) | collective-permute-done | bytes 65568 | tf_op jit(solution)/shard_map/ppermute | solution.py:176
  67.6 1.8 %collective-permute-start.24 = (f32[128,128]{1,0:T(8,128)S(1)}, f32[128,128]{1,0:T(8,128)S(1)}, u32[]{:S(2)}, u32[]{:S(2)}) collective-permute-start(f32[128,128]{1,0:T(8,128)S(1)} %get-tuple-element.75.j0), channel_id=1, source_target_pairs={{0,32},{8,40},{16,48},{24,56},{32,0},{40,8},{48,16},{56,24},{64,96... | collective-permute-start | bytes 196616 | tf_op jit(solution)/shard_map/ppermute | solution.py:176
  69.4 2.0 %collective-permute-start.25 = (f32[128,128]{1,0:T(8,128)S(1)}, f32[128,128]{1,0:T(8,128)S(1)}, u32[]{:S(2)}, u32[]{:S(2)}) collective-permute-start(f32[128,128]{1,0:T(8,128)S(1)} %get-tuple-element.75.j0), channel_id=1, source_target_pairs={{0,48},{8,56},{16,32},{24,40},{32,16},{40,24},{48,0},{56,8},{64,11... | collective-permute-start | bytes 196616 | tf_op jit(solution)/shard_map/ppermute | solution.py:176
  71.4 2.9 %collective-permute-start.26 = (f32[128,128]{1,0:T(8,128)S(1)}, f32[128,128]{1,0:T(8,128)S(1)}, u32[]{:S(2)}, u32[]{:S(2)}) collective-permute-start(f32[128,128]{1,0:T(8,128)S(1)} %get-tuple-element.74), channel_id=1, source_target_pairs={{0,196},{1,197},{2,198},{3,199},{4,192},{5,193},{6,194},{7,195},{8... | collective-permute-start | bytes 196616 | tf_op jit(solution)/shard_map/ppermute | solution.py:242
  74.3 2.6 %collective-permute-done.26 = f32[128,128]{1,0:T(8,128)S(1)} collective-permute-done((f32[128,128]{1,0:T(8,128)S(1)}, f32[128,128]{1,0:T(8,128)S(1)}, u32[]{:S(2)}, u32[]{:S(2)}) %collective-permute-start.26) | collective-permute-done | bytes 65568 | tf_op jit(solution)/shard_map/ppermute | solution.py:242
  77.0 2.7 %collective-permute-start.27 = (f32[2,128,128]{2,1,0:T(8,128)S(1)}, f32[2,128,128]{2,1,0:T(8,128)S(1)}, u32[]{:S(2)}, u32[]{:S(2)}) collective-permute-start(f32[2,128,128]{2,1,0:T(8,128)S(1)} %pad_maximum_fusion.1), channel_id=1, source_target_pairs={{0,8},{8,0},{16,24},{24,16},{32,40},{40,32},{48,56},{56,48},{64,72... | collective-permute-start | bytes 393224 | tf_op jit(solution)/shard_map/ppermute | solution.py:176
  82.6 1.9 %collective-permute-start.30 = (f32[128,128]{1,0:T(8,128)S(1)}, f32[128,128]{1,0:T(8,128)S(1)}, u32[]{:S(2)}, u32[]{:S(2)}) collective-permute-start(f32[128,128]{1,0:T(8,128)S(1)} %get-tuple-element.66), channel_id=1, source_target_pairs={{0,16},{8,24},{16,0},{24,8},{32,48},{40,56},{48,32},{56,40},{64,80... | collective-permute-start | bytes 196616 | tf_op jit(solution)/shard_map/ppermute | solution.py:176
  87.6 2.4 %collective-permute-start.34 = (f32[32,128]{0,1:T(8,128)S(1)}, f32[32,128]{0,1:T(8,128)S(1)}, u32[]{:S(2)}, u32[]{:S(2)}) collective-permute-start(f32[32,128]{0,1:T(8,128)S(1)} %get-tuple-element.95), channel_id=1, source_target_pairs={{0,64},{8,72},{16,80},{24,88},{32,96},{40,104},{48,112},{56,120},{... | collective-permute-start | bytes 49160 | tf_op jit(solution)/shard_map/ppermute | solution.py:176
  90.4 1.7 %collective-permute-start.36 = (f32[32,128]{0,1:T(8,128)S(1)}, f32[32,128]{0,1:T(8,128)S(1)}, u32[]{:S(2)}, u32[]{:S(2)}) collective-permute-start(f32[32,128]{0,1:T(8,128)S(1)} %get-tuple-element.93), channel_id=1, source_target_pairs={{0,192},{8,200},{16,208},{24,216},{32,224},{40,232},{48,240},{56,2... | collective-permute-start | bytes 49160 | tf_op jit(solution)/shard_map/ppermute | solution.py:176
  92.1 3.1 %collective-permute-start.29 = (f32[128,128]{1,0:T(8,128)S(1)}, f32[128,128]{1,0:T(8,128)S(1)}, u32[]{:S(2)}, u32[]{:S(2)}) collective-permute-start(f32[128,128]{1,0:T(8,128)S(1)} %fusion.6), channel_id=1, source_target_pairs={{0,3},{1,2},{2,1},{3,0},{4,7},{5,6},{6,5},{7,4},{8,11},{9,10},{10,... | collective-permute-start | bytes 196616 | tf_op jit(solution)/shard_map/ppermute | solution.py:179
  97.3 2.9 %collective-permute-start.37 = (f32[16,128]{0,1:T(8,128)S(1)}, f32[16,128]{0,1:T(8,128)S(1)}, u32[]{:S(2)}, u32[]{:S(2)}) collective-permute-start(f32[16,128]{0,1:T(8,128)S(1)} %get-tuple-element.92), channel_id=1, source_target_pairs={{0,8},{8,0},{16,24},{24,16},{32,40},{40,32},{48,56},{56,48},{64,72... | collective-permute-start | bytes 24584 | tf_op jit(solution)/shard_map/ppermute | solution.py:176
  (118 shorter events, 31.8 us)
Async XLA Ops:
  6.7 16.4 %all-to-all-start = ((f32[16,32,128]{2,1,0:T(8,128)}), f32[16,32,128]{2,1,0:T(8,128)S(1)}, u32[]{:S(2)}, u32[]{:S(2)}) async-start(f32[16,32,128]{2,1,0:T(8,128)} %broadcast_in_dim.10), calls=%async_computation | async-start | bytes 524288 | tf_op jit(solution)/shard_map/all_to_all | solution.py:196
  13.2 10.4 %collective-permute-start.1 = (f32[128,256]{1,0:T(8,128)S(1)}, f32[128,256]{1,0:T(8,128)S(1)}, u32[]{:S(2)}, u32[]{:S(2)}) collective-permute-start(f32[128,256]{1,0:T(8,128)S(1)} %bitcast.120), channel_id=1, source_target_pairs={{0,8},{8,0},{16,24},{24,16},{32,40},{40,32},{48,56},{56,48},{64,72... | collective-permute-start | bytes 393224 | tf_op jit(solution)/shard_map/ppermute | solution.py:176
  30.7 5.0 %collective-permute-start.9 = (f32[128,128]{1,0:T(8,128)S(1)}, f32[128,128]{1,0:T(8,128)S(1)}, u32[]{:S(2)}, u32[]{:S(2)}) collective-permute-start(f32[128,128]{1,0:T(8,128)S(1)} %add_add_fusion.3), channel_id=1, source_target_pairs={{0,192},{8,200},{16,208},{24,216},{32,224},{40,232},{48,240},{56,2... | collective-permute-start | bytes 196616 | tf_op jit(solution)/shard_map/ppermute | solution.py:176
  37.5 6.7 %collective-permute-start.11 = (f32[128,128]{1,0:T(8,128)S(1)}, f32[128,128]{1,0:T(8,128)S(1)}, u32[]{:S(2)}, u32[]{:S(2)}) collective-permute-start(f32[128,128]{1,0:T(8,128)S(1)} %multiply_add_fusion.3.j0), channel_id=1, source_target_pairs={{0,16},{8,24},{16,0},{24,8},{32,48},{40,56},{48,32},{56,40},{64,80... | collective-permute-start | bytes 196616 | tf_op jit(solution)/shard_map/ppermute | solution.py:176
  38.0 6.2 %collective-permute-start.12 = (f32[128,128]{1,0:T(8,128)S(1)}, f32[128,128]{1,0:T(8,128)S(1)}, u32[]{:S(2)}, u32[]{:S(2)}) collective-permute-start(f32[128,128]{1,0:T(8,128)S(1)} %multiply_add_fusion.3.j0), channel_id=1, source_target_pairs={{0,32},{8,40},{16,48},{24,56},{32,0},{40,8},{48,16},{56,24},{64,96... | collective-permute-start | bytes 196616 | tf_op jit(solution)/shard_map/ppermute | solution.py:176
  41.4 8.2 %collective-permute-start.10 = (f32[128,128]{1,0:T(8,128)S(1)}, f32[128,128]{1,0:T(8,128)S(1)}, u32[]{:S(2)}, u32[]{:S(2)}) collective-permute-start(f32[128,128]{1,0:T(8,128)S(1)} %multiply_add_fusion.3.j0), channel_id=1, source_target_pairs={{0,196},{1,197},{2,198},{3,199},{4,192},{5,193},{6,194},{7,195},{8... | collective-permute-start | bytes 196616 | tf_op jit(solution)/shard_map/ppermute | solution.py:242
  46.4 12.2 %collective-permute-start.19 = (f32[128,128]{1,0:T(8,128)S(1)}, f32[128,128]{1,0:T(8,128)S(1)}, u32[]{:S(2)}, u32[]{:S(2)}) collective-permute-start(f32[128,128]{1,0:T(8,128)S(1)} %get-tuple-element.56), channel_id=1, source_target_pairs={{0,48},{8,56},{16,32},{24,40},{32,16},{40,24},{48,0},{56,8},{64,11... | collective-permute-start | bytes 196616 | tf_op jit(solution)/shard_map/ppermute | solution.py:176
  47.1 11.4 %collective-permute-start.18 = (f32[128,128]{1,0:T(8,128)S(1)}, f32[128,128]{1,0:T(8,128)S(1)}, u32[]{:S(2)}, u32[]{:S(2)}) collective-permute-start(f32[128,128]{1,0:T(8,128)S(1)} %get-tuple-element.55), channel_id=1, source_target_pairs={{0,32},{8,40},{16,48},{24,56},{32,0},{40,8},{48,16},{56,24},{64,96... | collective-permute-start | bytes 196616 | tf_op jit(solution)/shard_map/ppermute | solution.py:176
  47.2 11.4 %collective-permute-start.17 = (f32[128,128]{1,0:T(8,128)S(1)}, f32[128,128]{1,0:T(8,128)S(1)}, u32[]{:S(2)}, u32[]{:S(2)}) collective-permute-start(f32[128,128]{1,0:T(8,128)S(1)} %get-tuple-element.54), channel_id=1, source_target_pairs={{0,16},{8,24},{16,0},{24,8},{32,48},{40,56},{48,32},{56,40},{64,80... | collective-permute-start | bytes 196616 | tf_op jit(solution)/shard_map/ppermute | solution.py:176
  49.6 7.4 %collective-permute-start.14 = (f32[2,128,128]{2,1,0:T(8,128)S(1)}, f32[2,128,128]{2,1,0:T(8,128)S(1)}, u32[]{:S(2)}, u32[]{:S(2)}) collective-permute-start(f32[2,128,128]{2,1,0:T(8,128)S(1)} %pad_maximum_fusion), channel_id=1, source_target_pairs={{0,8},{8,0},{16,24},{24,16},{32,40},{40,32},{48,56},{56,48},{64,72... | collective-permute-start | bytes 393224 | tf_op jit(solution)/shard_map/ppermute | solution.py:176
  57.2 5.1 %collective-permute-start.15 = (f32[2,128,128]{2,1,0:T(8,128)S(1)}, f32[2,128,128]{2,1,0:T(8,128)S(1)}, u32[]{:S(2)}, u32[]{:S(2)}) collective-permute-start(f32[2,128,128]{2,1,0:T(8,128)S(1)} %slice.137), channel_id=1, source_target_pairs={{0,1},{1,0},{2,3},{3,2},{4,5},{5,4},{6,7},{7,6},{8,9},{9,8},{10,11... | collective-permute-start | bytes 393224 | tf_op jit(solution)/shard_map/ppermute | solution.py:179
  58.6 6.2 %collective-permute-start.22 = (f32[128,128]{1,0:T(8,128)S(1)}, f32[128,128]{1,0:T(8,128)S(1)}, u32[]{:S(2)}, u32[]{:S(2)}) collective-permute-start(f32[128,128]{1,0:T(8,128)S(1)} %add_add_fusion.2), channel_id=1, source_target_pairs={{0,192},{8,200},{16,208},{24,216},{32,224},{40,232},{48,240},{56,2... | collective-permute-start | bytes 196616 | tf_op jit(solution)/shard_map/ppermute | solution.py:176
  59.9 7.5 %collective-permute-start.21 = (f32[128,128]{1,0:T(8,128)S(1)}, f32[128,128]{1,0:T(8,128)S(1)}, u32[]{:S(2)}, u32[]{:S(2)}) collective-permute-start(f32[128,128]{1,0:T(8,128)S(1)} %add_add_fusion.2), channel_id=1, source_target_pairs={{0,128},{8,136},{16,144},{24,152},{32,160},{40,168},{48,176},{56,1... | collective-permute-start | bytes 196616 | tf_op jit(solution)/shard_map/ppermute | solution.py:176
  60.9 6.5 %collective-permute-start.20 = (f32[128,128]{1,0:T(8,128)S(1)}, f32[128,128]{1,0:T(8,128)S(1)}, u32[]{:S(2)}, u32[]{:S(2)}) collective-permute-start(f32[128,128]{1,0:T(8,128)S(1)} %add_add_fusion.2), channel_id=1, source_target_pairs={{0,64},{8,72},{16,80},{24,88},{32,96},{40,104},{48,112},{56,120},{... | collective-permute-start | bytes 196616 | tf_op jit(solution)/shard_map/ppermute | solution.py:176
  62.3 5.2 %collective-permute-start.16 = (f32[128,128]{1,0:T(8,128)S(1)}, f32[128,128]{1,0:T(8,128)S(1)}, u32[]{:S(2)}, u32[]{:S(2)}) collective-permute-start(f32[128,128]{1,0:T(8,128)S(1)} %fusion.9), channel_id=1, source_target_pairs={{0,3},{1,2},{2,1},{3,0},{4,7},{5,6},{6,5},{7,4},{8,11},{9,10},{10,... | collective-permute-start | bytes 196616 | tf_op jit(solution)/shard_map/ppermute | solution.py:179
  67.5 9.5 %collective-permute-start.23 = (f32[128,128]{1,0:T(8,128)S(1)}, f32[128,128]{1,0:T(8,128)S(1)}, u32[]{:S(2)}, u32[]{:S(2)}) collective-permute-start(f32[128,128]{1,0:T(8,128)S(1)} %get-tuple-element.75.j0), channel_id=1, source_target_pairs={{0,16},{8,24},{16,0},{24,8},{32,48},{40,56},{48,32},{56,40},{64,80... | collective-permute-start | bytes 196616 | tf_op jit(solution)/shard_map/ppermute | solution.py:176
  67.6 9.4 %collective-permute-start.24 = (f32[128,128]{1,0:T(8,128)S(1)}, f32[128,128]{1,0:T(8,128)S(1)}, u32[]{:S(2)}, u32[]{:S(2)}) collective-permute-start(f32[128,128]{1,0:T(8,128)S(1)} %get-tuple-element.75.j0), channel_id=1, source_target_pairs={{0,32},{8,40},{16,48},{24,56},{32,0},{40,8},{48,16},{56,24},{64,96... | collective-permute-start | bytes 196616 | tf_op jit(solution)/shard_map/ppermute | solution.py:176
  69.4 7.6 %collective-permute-start.25 = (f32[128,128]{1,0:T(8,128)S(1)}, f32[128,128]{1,0:T(8,128)S(1)}, u32[]{:S(2)}, u32[]{:S(2)}) collective-permute-start(f32[128,128]{1,0:T(8,128)S(1)} %get-tuple-element.75.j0), channel_id=1, source_target_pairs={{0,48},{8,56},{16,32},{24,40},{32,16},{40,24},{48,0},{56,8},{64,11... | collective-permute-start | bytes 196616 | tf_op jit(solution)/shard_map/ppermute | solution.py:176
  71.4 5.5 %collective-permute-start.26 = (f32[128,128]{1,0:T(8,128)S(1)}, f32[128,128]{1,0:T(8,128)S(1)}, u32[]{:S(2)}, u32[]{:S(2)}) collective-permute-start(f32[128,128]{1,0:T(8,128)S(1)} %get-tuple-element.74), channel_id=1, source_target_pairs={{0,196},{1,197},{2,198},{3,199},{4,192},{5,193},{6,194},{7,195},{8... | collective-permute-start | bytes 196616 | tf_op jit(solution)/shard_map/ppermute | solution.py:242
  81.1 11.0 %collective-permute-start.28 = (f32[2,128,128]{2,1,0:T(8,128)S(1)}, f32[2,128,128]{2,1,0:T(8,128)S(1)}, u32[]{:S(2)}, u32[]{:S(2)}) collective-permute-start(f32[2,128,128]{2,1,0:T(8,128)S(1)} %slice.120), channel_id=1, source_target_pairs={{0,1},{1,0},{2,3},{3,2},{4,5},{5,4},{6,7},{7,6},{8,9},{9,8},{10,11... | collective-permute-start | bytes 393224 | tf_op jit(solution)/shard_map/ppermute | solution.py:179
  84.6 10.7 %collective-permute-start.33 = (f32[8,256]{1,0:T(8,128)S(1)}, f32[8,256]{1,0:T(8,128)S(1)}, u32[]{:S(2)}, u32[]{:S(2)}) collective-permute-start(f32[8,256]{1,0:T(8,128)S(1)} %get-tuple-element.97), channel_id=1, source_target_pairs={{0,8},{8,0},{16,24},{24,16},{32,40},{40,32},{48,56},{56,48},{64,72... | collective-permute-start | bytes 24584 | tf_op jit(solution)/shard_map/ppermute | solution.py:176
  87.6 8.3 %collective-permute-start.34 = (f32[32,128]{0,1:T(8,128)S(1)}, f32[32,128]{0,1:T(8,128)S(1)}, u32[]{:S(2)}, u32[]{:S(2)}) collective-permute-start(f32[32,128]{0,1:T(8,128)S(1)} %get-tuple-element.95), channel_id=1, source_target_pairs={{0,64},{8,72},{16,80},{24,88},{32,96},{40,104},{48,112},{56,120},{... | collective-permute-start | bytes 49160 | tf_op jit(solution)/shard_map/ppermute | solution.py:176
  89.9 5.9 %collective-permute-start.35 = (f32[32,128]{0,1:T(8,128)S(1)}, f32[32,128]{0,1:T(8,128)S(1)}, u32[]{:S(2)}, u32[]{:S(2)}) collective-permute-start(f32[32,128]{0,1:T(8,128)S(1)} %get-tuple-element.94), channel_id=1, source_target_pairs={{0,128},{8,136},{16,144},{24,152},{32,160},{40,168},{48,176},{56,1... | collective-permute-start | bytes 49160 | tf_op jit(solution)/shard_map/ppermute | solution.py:176
  90.4 5.5 %collective-permute-start.36 = (f32[32,128]{0,1:T(8,128)S(1)}, f32[32,128]{0,1:T(8,128)S(1)}, u32[]{:S(2)}, u32[]{:S(2)}) collective-permute-start(f32[32,128]{0,1:T(8,128)S(1)} %get-tuple-element.93), channel_id=1, source_target_pairs={{0,192},{8,200},{16,208},{24,216},{32,224},{40,232},{48,240},{56,2... | collective-permute-start | bytes 49160 | tf_op jit(solution)/shard_map/ppermute | solution.py:176
  (19 other events, 68.6 us)
